TPU v7x, 32 devices: a whole 2x2x4 slice. The times are simulated.
32 devices in a mesh: dp: 4 (over z), ctx: 4 (over y, x), tp: 2 (over core).
Axes of the slice: x: 2, y: 2, z: 4, core: 2. Of those that a mesh axis runs over, the one named last changes fastest.
Arguments:
- stream_in: bfloat16 [4, 1024, 1024], P('dp', 'ctx'), may hold values from -6 to 6
- norm_gain: bfloat16 [1024], P('dp'), may hold values from 0.5 to 1.5
- in_weight: bfloat16 [2, 1024, 2048], P(None, 'dp', 'tp'), may hold values from -0.1875 to 0.1875
- out_weight: bfloat16 [2048, 1024], P('tp', 'dp'), may hold values from -0.125 to 0.125
- xproj_weight: bfloat16 [96, 2048], P('dp', 'tp'), may hold values from -0.125 to 0.125
- dt_weight: bfloat16 [64, 2048], P('dp', 'tp'), may hold values from -0.75 to 0.75
- a_log: bfloat16 [16, 2048], P('dp', 'tp'), may hold values from -6 to 0.69921875
- convolution_weight: bfloat16 [4, 2, 1024], P(None, 'tp', 'dp'), may hold values from -3 to 3
- convolution_bias: bfloat16 [2, 1024], P('tp', 'dp'), may hold values from -3 to 3
- step_size_bias: bfloat16 [2, 1024], P('tp', 'dp'), may hold values from -6 to -3
- skip_term_scale: bfloat16 [2, 1024], P('tp', 'dp'), may hold values from 0.5 to 1.5
- seg_ids: int32 [4, 1024], P('dp', 'ctx'), may hold values from 0 to 15, as said below
- pad_mask: int32 [4, 1024], P('dp', 'ctx'), may hold values from 0 to 1, as said below
- out_grad: bfloat16 [4, 1024, 1024], P('dp', 'ctx'), may hold values from -6 to 6
Outputs:
- stream_out: bfloat16 [4, 1024, 1024], P('dp', 'ctx')
- stream_grad: float32 [4, 1024, 1024], P('dp', 'ctx')
- norm_gain_grad: float32 [1024], P('dp')
- input_weight_gradient: float32 [2, 1024, 2048], P(None, 'dp', 'tp')
- out_weight_grad: float32 [2048, 1024], P('tp', 'dp')
- xproj_grad: float32 [96, 2048], P('dp', 'tp')
- dt_weight_grad: float32 [64, 2048], P('dp', 'tp')
- a_log_grad: float32 [16, 2048], P('dp', 'tp')
- conv_weight_grad: float32 [4, 2, 1024], P(None, 'tp', 'dp')
- conv_bias_grad: float32 [2, 1024], P('tp', 'dp')
- dt_bias_grad: float32 [2, 1024], P('tp', 'dp')
- skip_gain_grad: float32 [2, 1024], P('tp', 'dp')
Inputs may be any that keep to these rules, and one draw needn't show every extreme that they name: `seg_ids`: along each sequence the document number starts at 0 and never falls; the last byte of every sequence has number 16 - 1; a document may span many spans of positions. `pad_mask`: in each sequence the ones form a leading run and at least one trailing byte is 0; at most 1024 // 8 bytes of a sequence are 0.
All inputs are finite; a program needn't handle non-finite values.
Results may differ from a plain program's by a relative error of at most 0.011.
Values may be sent and summed in bfloat16 or wider, within the bound.
A program may use at most 256 MiB of HBM per device.

v0:
```python
import math

import jax
import jax.numpy as jnp
from jax import lax
from jax.experimental import pallas as pl
from jax.experimental.pallas import tpu as pltpu
from jax.sharding import PartitionSpec as P

EPS = 1e-05
VMEM_LIMIT = 63 * 2**20


def from_behind(x, axis, by):
    count = lax.axis_size(axis)
    pairs = [(i, i + by) for i in range(count) if 0 <= i + by < count]
    return lax.ppermute(x, axis, pairs)


def entering(x, axis, combine, identity, reverse):
    count, position = (lax.axis_size(axis), lax.axis_index(axis))
    everything = jax.tree.map(
        lambda part, kind: lax.all_gather(part.astype(kind), axis), x, (jnp.bfloat16, jnp.bfloat16)
    )
    start = jax.tree.map(
        lambda part, zero: jnp.broadcast_to(jnp.asarray(zero, part.dtype), part.shape), x, identity
    )

    def step(k, before):
        at = count - 1 - k if reverse else k
        reached = at > position if reverse else at < position
        new = combine(
            before, jax.tree.map(lambda part, own: part[at].astype(own.dtype), everything, x)
        )
        return jax.tree.map(lambda a, b: jnp.where(reached, a, b), new, before)

    return lax.fori_loop(0, count, step, start)


def silu_slope(value):
    sigma = jax.nn.sigmoid(value)
    return sigma * (1.0 + value * (1.0 - sigma))


def link(first, second):
    return (first[0] * second[0], first[1] * second[0] + second[1])


def chain_prefix(decay, drive, backward):
    return lax.associative_scan(link, (decay, drive), reverse=backward, axis=1)


def shards(
    stream_in,
    norm_gain,
    in_weight,
    out_weight,
    xproj_weight,
    dt_weight,
    a_log,
    convolution_weight,
    convolution_bias,
    step_size_bias,
    skip_term_scale,
    seg_ids,
    pad_mask,
    out_grad,
):
    gathered = (
        lax.all_gather(norm_gain, "dp", axis=0, tiled=True),
        lax.all_gather(in_weight, "dp", axis=1, tiled=True),
        lax.all_gather(out_weight, "dp", axis=1, tiled=True),
        lax.all_gather(xproj_weight, "dp", axis=0, tiled=True),
        lax.all_gather(dt_weight, "dp", axis=0, tiled=True),
        lax.all_gather(a_log, "dp", axis=0, tiled=True),
        lax.all_gather(convolution_weight, "dp", axis=2, tiled=True),
        lax.all_gather(convolution_bias, "dp", axis=1, tiled=True),
        lax.all_gather(step_size_bias, "dp", axis=1, tiled=True),
        lax.all_gather(skip_term_scale, "dp", axis=1, tiled=True),
    )
    (
        gain_full,
        win_full,
        wout_full,
        xproj_full,
        dtw_full,
        alog_full,
        convw_full,
        convb_full,
        dtb_full,
        skip_full,
    ) = gathered
    seq_count, tok_count, model_width = stream_in.shape
    channels = win_full.shape[2]
    low_dims = dtw_full.shape[0]
    states = alog_full.shape[0]
    kernel = convw_full.shape[0]
    conv_lag = kernel - 1
    row_count = seq_count * tok_count
    block_len = math.gcd(tok_count, 128)
    block_count = tok_count // block_len
    gain_vec = gain_full.astype(jnp.float32)
    conv_taps = convw_full.reshape(kernel, channels).astype(jnp.float32)
    conv_shift = convb_full.reshape(channels).astype(jnp.float32)
    dt_shift = dtb_full.reshape(channels).astype(jnp.float32)
    skip_vec = skip_full.reshape(channels).astype(jnp.float32)
    a_neg = -jnp.exp(alog_full.astype(jnp.float32))

    def to_blocks(array):
        shaped = array.reshape((seq_count, block_count, block_len) + array.shape[2:])
        return jnp.moveaxis(shaped, 1, 0)

    def from_blocks(array):
        return jnp.moveaxis(array, 0, 1).reshape((seq_count, tok_count) + array.shape[3:])

    def decay_of(dt_block, keep_block):
        return jnp.exp(dt_block[:, :, None, :] * a_neg) * keep_block[:, :, None, None]

    def drive_of(dt_block, act_block, b_block):
        return (dt_block * act_block)[:, :, None, :] * b_block[:, :, :, None]

    def reverse_terms(decay, rhs, carry_in):
        shifted = jnp.concatenate([decay[:, 1:], jnp.zeros_like(decay[:, :1])], axis=1)
        rhs = rhs.at[:, -1].add(carry_in)
        _, grads = chain_prefix(shifted, rhs, True)
        return (grads, decay[:, 0] * grads[:, 0])

    stream = stream_in.astype(jnp.float32)
    rstd = lax.rsqrt(jnp.mean(stream * stream, axis=2, keepdims=True) + EPS)
    normed = (stream * rstd * gain_vec).astype(jnp.bfloat16)
    normed_flat = normed.reshape(row_count, model_width)
    projected = jnp.einsum(
        "rd,kdc->krc", normed_flat, win_full, preferred_element_type=jnp.float32
    ).astype(jnp.bfloat16)
    inner = projected[0].reshape(seq_count, tok_count, channels)
    gate_vals = projected[1].astype(jnp.float32).reshape(seq_count, tok_count, channels)
    seg_low = seg_ids.astype(jnp.bfloat16)
    prev_inner, prev_seg = from_behind(
        (inner[:, tok_count - conv_lag :], seg_low[:, tok_count - conv_lag :]), "ctx", 1
    )
    inner_vals = inner.astype(jnp.float32)
    prev_vals = prev_inner.astype(jnp.float32)
    seg_float = seg_ids.astype(jnp.float32)
    prev_segf = prev_seg.astype(jnp.float32)
    windows = []
    same_list = []
    pre = jnp.zeros((seq_count, tok_count, channels), jnp.float32) + conv_shift
    for offset in range(kernel):
        if offset == 0:
            window = inner_vals
            seg_window = seg_float
        else:
            window = jnp.concatenate(
                [prev_vals[:, conv_lag - offset :], inner_vals[:, : tok_count - offset]], axis=1
            )
            seg_window = jnp.concatenate(
                [prev_segf[:, conv_lag - offset :], seg_float[:, : tok_count - offset]], axis=1
            )
        same = (seg_window == seg_float).astype(jnp.float32)
        windows.append(window)
        same_list.append(same)
        pre = pre + conv_taps[conv_lag - offset] * window * same[:, :, None]
    keep = same_list[1]
    act = (pre * jax.nn.sigmoid(pre)).astype(jnp.bfloat16)
    act_flat = act.reshape(row_count, channels)
    act_vals = act.astype(jnp.float32)
    mixed_part = jnp.einsum("rc,wc->rw", act_flat, xproj_full, preferred_element_type=jnp.float32)
    mixed = lax.psum(mixed_part, "tp")
    low_rank = mixed[:, :low_dims].astype(jnp.bfloat16)
    b_in = mixed[:, low_dims : low_dims + states].reshape(seq_count, tok_count, states)
    c_out = mixed[:, low_dims + states :].reshape(seq_count, tok_count, states)
    dt_arg = (
        jnp.dot(low_rank, dtw_full, preferred_element_type=jnp.float32).reshape(
            seq_count, tok_count, channels
        )
        + dt_shift
    )
    dt_values = jax.nn.softplus(dt_arg)

    def forward_block(carry, piece):
        start, through = carry
        dt_block, act_block, b_block, c_block, keep_block = piece
        decay = decay_of(dt_block, keep_block)
        prods, local = chain_prefix(decay, drive_of(dt_block, act_block, b_block), False)
        hidden = local + prods * start[:, None]
        outputs = jnp.sum(c_block[:, :, :, None] * hidden, axis=2)
        return ((hidden[:, -1], through * prods[:, -1]), (outputs, start, through))

    zero_state = jnp.zeros((seq_count, states, channels), jnp.float32)
    one_state = jnp.ones_like(zero_state)
    dt_blocks = to_blocks(dt_values)
    act_blocks = to_blocks(act_vals)
    b_blocks = to_blocks(b_in)
    c_blocks = to_blocks(c_out)
    keep_blocks = to_blocks(keep)
    (last_state, through), (y_blocks, local_starts, befores) = lax.scan(
        forward_block,
        (zero_state, one_state),
        (dt_blocks, act_blocks, b_blocks, c_blocks, keep_blocks),
    )
    _, entry_state = entering((through, last_state), "ctx", link, (one_state, zero_state), False)
    cum_dt = jnp.cumsum(dt_values, axis=1)
    alive = jnp.cumprod(keep, axis=1)
    cum_blocks = to_blocks(cum_dt)

    def correct(piece):
        cum_block, c_block, alive_block = piece
        carried = jnp.exp(cum_block[:, :, None, :] * a_neg) * entry_state[:, None]
        return alive_block[:, :, None] * jnp.sum(c_block[:, :, :, None] * carried, axis=2)

    corrections = from_blocks(lax.map(correct, (cum_blocks, c_blocks, to_blocks(alive))))
    y_total = from_blocks(y_blocks) + corrections + skip_vec * act_vals
    gate_act = gate_vals * jax.nn.sigmoid(gate_vals)
    gated_flat = (y_total * gate_act).astype(jnp.bfloat16).reshape(row_count, channels)
    branch_part = jnp.dot(gated_flat, wout_full, preferred_element_type=jnp.float32)
    branch = (
        lax.psum(branch_part.astype(jnp.bfloat16), "tp")
        .astype(jnp.float32)
        .reshape(seq_count, tok_count, model_width)
    )
    mask_float = pad_mask.astype(jnp.float32)
    stream_out = (stream + mask_float[:, :, None] * branch).astype(jnp.bfloat16)
    masked_flat = (out_grad * pad_mask[:, :, None].astype(jnp.bfloat16)).reshape(
        row_count, model_width
    )
    grad_wout = jnp.einsum("rc,rd->cd", gated_flat, masked_flat, preferred_element_type=jnp.float32)
    grad_gated = jnp.einsum(
        "rd,cd->rc", masked_flat, wout_full, preferred_element_type=jnp.float32
    ).reshape(seq_count, tok_count, channels)
    grad_y = grad_gated * gate_act
    grad_gate = (grad_gated * y_total * silu_slope(gate_vals)).astype(jnp.bfloat16)
    grad_skip = jnp.sum(grad_y * act_vals, axis=(0, 1))
    gy_blocks = to_blocks(grad_y)
    true_starts = local_starts + befores * entry_state[None]

    def back_core(carry_in, piece):
        dt_block, act_block, b_block, c_block, keep_block, gy_block, start = piece
        decay = decay_of(dt_block, keep_block)
        prods, local = chain_prefix(decay, drive_of(dt_block, act_block, b_block), False)
        hidden = local + prods * start[:, None]
        earlier = jnp.concatenate([start[:, None], hidden[:, :-1]], axis=1)
        grads, carry_out = reverse_terms(
            decay, c_block[:, :, :, None] * gy_block[:, :, None, :], carry_in
        )
        stepped = earlier * decay
        weighted = grads * stepped
        along_b = jnp.sum(grads * b_block[:, :, :, None], axis=2)
        grad_dt = jnp.sum(weighted * a_neg, axis=2) + along_b * act_block
        grad_act = along_b * dt_block
        grad_b = jnp.sum(grads * (dt_block * act_block)[:, :, None, :], axis=3)
        grad_c = jnp.sum(gy_block[:, :, None, :] * hidden, axis=3)
        return (carry_out, weighted, stepped, (grad_dt, grad_act, grad_b, grad_c))

    back_pieces = (dt_blocks, act_blocks, b_blocks, c_blocks, keep_blocks, gy_blocks, true_starts)
    zero_acc = jnp.zeros((states, channels), jnp.float32)
    cum_end = cum_dt[:, -1]
    suffix = jnp.flip(jnp.cumprod(jnp.flip(keep, axis=1), axis=1), axis=1)
    rest = jnp.concatenate([suffix[:, 1:], jnp.ones((seq_count, 1), jnp.float32)], axis=1)
    rest_blocks = to_blocks(rest)

    def reach_of(cum_block, rest_block):
        return (
            jnp.exp((cum_end[:, None, None, :] - cum_block[:, :, None, :]) * a_neg)
            * rest_block[:, :, None, None]
        )

    def kept_back(carry, piece):
        carry_in, a_acc, q_acc = carry
        core_piece = piece[:7]
        carry_out, weighted, stepped, terms = back_core(carry_in, core_piece)
        dt_block = core_piece[0]
        along = stepped * reach_of(piece[7], piece[8])
        a_acc = a_acc + jnp.sum(weighted * dt_block[:, :, None, :], axis=(0, 1))
        q_acc = q_acc + jnp.sum(along * dt_block[:, :, None, :], axis=1)
        return ((carry_out, a_acc, q_acc), terms + (along,))

    (edge_grad, a_local, q_total), (base_dt, base_act, base_b, grad_c_blocks, along_blocks) = (
        lax.scan(
            kept_back,
            (zero_state, zero_acc, zero_state),
            back_pieces + (cum_blocks, rest_blocks),
            reverse=True,
        )
    )
    _, after_grad = entering((through, edge_grad), "ctx", link, (one_state, zero_state), True)

    def adjust(piece):
        dt_block, act_block, b_block, cum_block, rest_block, along = piece
        extra = reach_of(cum_block, rest_block) * after_grad[:, None]
        along_b = jnp.sum(extra * b_block[:, :, :, None], axis=2)
        grad_dt = jnp.sum(along * after_grad[:, None] * a_neg, axis=2) + along_b * act_block
        grad_act = along_b * dt_block
        grad_b = jnp.sum(extra * (dt_block * act_block)[:, :, None, :], axis=3)
        return (grad_dt, grad_act, grad_b)

    add_dt, add_act, add_b = lax.map(
        adjust, (dt_blocks, act_blocks, b_blocks, cum_blocks, rest_blocks, along_blocks)
    )
    grad_dt_blocks = base_dt + add_dt
    grad_act_blocks = base_act + add_act
    grad_b_blocks = base_b + add_b
    a_total = a_local + jnp.sum(q_total * after_grad, axis=0)
    grad_lin = from_blocks(grad_dt_blocks) * jax.nn.sigmoid(dt_arg)
    grad_dtb = jnp.sum(grad_lin, axis=(0, 1))
    grad_lin_low = grad_lin.reshape(row_count, channels).astype(jnp.bfloat16)
    grad_dtw = jnp.einsum("rk,rc->kc", low_rank, grad_lin_low, preferred_element_type=jnp.float32)
    grad_rank = jnp.einsum("rc,kc->rk", grad_lin_low, dtw_full, preferred_element_type=jnp.float32)
    grad_mixed_part = jnp.concatenate(
        [
            grad_rank,
            from_blocks(grad_b_blocks).reshape(row_count, states),
            from_blocks(grad_c_blocks).reshape(row_count, states),
        ],
        axis=1,
    )
    grad_mixed = lax.psum(grad_mixed_part, "tp").astype(jnp.bfloat16)
    grad_xproj = jnp.einsum("rw,rc->wc", grad_mixed, act_flat, preferred_element_type=jnp.float32)
    grad_act_total = (
        grad_y * skip_vec
        + from_blocks(grad_act_blocks)
        + jnp.dot(grad_mixed, xproj_full, preferred_element_type=jnp.float32).reshape(
            seq_count, tok_count, channels
        )
    )
    grad_pre = grad_act_total * silu_slope(pre)
    grad_convb = jnp.sum(grad_pre, axis=(0, 1))
    tap_grads = [None] * kernel
    grad_inner = jnp.zeros((seq_count, tok_count, channels), jnp.float32)
    tail_grad = jnp.zeros((seq_count, conv_lag, channels), jnp.float32)
    for offset in range(kernel):
        weighted_pre = grad_pre * same_list[offset][:, :, None]
        tap_grads[conv_lag - offset] = jnp.sum(weighted_pre * windows[offset], axis=(0, 1))
        scaled_pre = weighted_pre * conv_taps[conv_lag - offset]
        if offset == 0:
            grad_inner = grad_inner + scaled_pre
        else:
            grad_inner = grad_inner + jnp.concatenate(
                [scaled_pre[:, offset:], jnp.zeros((seq_count, offset, channels), jnp.float32)],
                axis=1,
            )
            tail_grad = tail_grad.at[:, conv_lag - offset :].add(scaled_pre[:, :offset])
    grad_convw = jnp.stack(tap_grads)
    sent_back = from_behind(tail_grad, "ctx", -1)
    grad_inner = grad_inner.at[:, tok_count - conv_lag :].add(sent_back)
    grad_proj = jnp.stack(
        [
            grad_inner.astype(jnp.bfloat16).reshape(row_count, channels),
            grad_gate.reshape(row_count, channels),
        ]
    )
    grad_win = jnp.einsum("rd,krc->kdc", normed_flat, grad_proj, preferred_element_type=jnp.float32)
    grad_norm_part = jnp.einsum(
        "krc,kdc->rd", grad_proj, win_full, preferred_element_type=jnp.float32
    )
    grad_norm = lax.psum(grad_norm_part, "tp").reshape(seq_count, tok_count, model_width)
    grad_gain = jnp.sum(grad_norm * stream * rstd, axis=(0, 1))
    scaled = grad_norm * gain_vec
    stream_grad = (
        out_grad.astype(jnp.float32)
        + rstd * scaled
        - stream * (rstd * rstd * rstd) * jnp.mean(scaled * stream, axis=2, keepdims=True)
    )
    grad_alog = a_total * a_neg
    local_grads = (
        grad_gain,
        grad_win,
        grad_wout,
        grad_xproj,
        grad_dtw,
        grad_alog,
        grad_convw.reshape(kernel, 1, channels),
        grad_convb.reshape(1, channels),
        grad_dtb.reshape(1, channels),
        grad_skip.reshape(1, channels),
    )
    summed = lax.psum(
        (
            local_grads[0],
            local_grads[1],
            local_grads[2],
            local_grads[3],
            local_grads[4],
            local_grads[5],
            local_grads[6],
            local_grads[7],
            local_grads[8],
            local_grads[9],
        ),
        "ctx",
    )
    owned = (
        lax.psum_scatter(summed[0], "dp", scatter_dimension=0, tiled=True),
        lax.psum_scatter(summed[1], "dp", scatter_dimension=1, tiled=True),
        lax.psum_scatter(summed[2], "dp", scatter_dimension=1, tiled=True),
        lax.psum_scatter(summed[3], "dp", scatter_dimension=0, tiled=True),
        lax.psum_scatter(summed[4], "dp", scatter_dimension=0, tiled=True),
        lax.psum_scatter(summed[5], "dp", scatter_dimension=0, tiled=True),
        lax.psum_scatter(summed[6], "dp", scatter_dimension=2, tiled=True),
        lax.psum_scatter(summed[7], "dp", scatter_dimension=1, tiled=True),
        lax.psum_scatter(summed[8], "dp", scatter_dimension=1, tiled=True),
        lax.psum_scatter(summed[9], "dp", scatter_dimension=1, tiled=True),
    )
    return (
        stream_out,
        stream_grad,
        owned[0],
        owned[1],
        owned[2],
        owned[3],
        owned[4],
        owned[5],
        owned[6],
        owned[7],
        owned[8],
        owned[9],
    )


F32 = jnp.float32
BF16 = jnp.bfloat16
MESH = pl.DeviceIdType.MESH
LOG2E = math.log2(math.e)
LN2 = math.log(2.0)
KILL = 1e30
SUB = 8
LANES = 128
PAD = 24
ROWS = 64
XP, DTW, ALOG, CONVW, CONVB, DTB, SKIP, GAIN = 0, 24, 40, 44, 48, 49, 50, 51
NT = (((1,), (1,)), ((), ()))
TN = (((0,), (0,)), ((), ()))


def dot(a, b):
    return jnp.dot(a, b, preferred_element_type=F32)


def dot_nt(a, b):
    return lax.dot_general(a, b, NT, preferred_element_type=F32)


def dot_tn(a, b):
    return lax.dot_general(a, b, TN, preferred_element_type=F32)


def at8(start, size):
    return pl.ds(pl.multiple_of(start, 8), size)


def one_less_exp(v):
    series = v * (1.0 - v * (0.5 - v * (1.0 / 6.0 - v * (1.0 / 24.0 - v * (1.0 / 120.0)))))
    return jnp.where(v < 0.1, series, 1.0 - jnp.exp(-v))


def prefix_of(ends, prods):
    row = lax.broadcasted_iota(jnp.int32, ends.shape, 0)
    for gap in (1, 2, 4):
        ok = row >= gap
        ends = ends + prods * jnp.where(ok, pltpu.roll(ends, gap, 0), 0.0)
        prods = prods * jnp.where(ok, pltpu.roll(prods, gap, 0), 1.0)
    return jnp.where(row >= 1, pltpu.roll(ends, 1, 0), 0.0)


def suffix_of(ends, prods):
    row = lax.broadcasted_iota(jnp.int32, ends.shape, 0)
    for gap in (1, 2, 4):
        ok = row < SUB - gap
        ends = ends + prods * jnp.where(ok, pltpu.roll(ends, SUB - gap, 0), 0.0)
        prods = prods * jnp.where(ok, pltpu.roll(prods, SUB - gap, 0), 1.0)
    return jnp.where(row < SUB - 1, pltpu.roll(ends, SUB - 1, 0), 0.0)


def fused_kernel(
    x_ref, og_ref, win_ref, wout_ref, xproj_ref, dtw_ref, alog_ref, convw_ref, convb_ref, dtb_ref,
    skip_ref, gain_ref, seg_ref, mask_ref,
    so_out, sg_out, wg_out, wo_out, sm_out, cv_out, gg_out,
    xf, mg, w_s, wo_s, pk_f, pk_s, segs, segp, maskc, nat, inner, slope, act, gate, dt, yg, y,
    bc, h, a2b, st, gin, cum, alg, full, full2, mp, sum_a, recv_a, recv_b, xp, dtwp,
    big_send, big_keep, big_recv, big_rb, gpart, zrecv, gres, gnat, znat, spart, srecv, sfull, sown, ggs,
    sg_s, ssem, rsem, lsem,
):
    z, c, k = lax.axis_index("dp"), lax.axis_index("ctx"), lax.axis_index("tp")
    nz = lax.axis_size("dp")
    px, py = lax.rem(c, 2), c // 2
    sib = (z, c, 1 - k)
    plane = [None, py * 2 + (1 - px), (1 - py) * 2 + px, (1 - py) * 2 + (1 - px)]
    peers = [None] + [(z, plane[p], k) for p in (1, 2, 3)]
    toward = [None] + [lax.rem(z + d, nz) for d in (1, 2, 3)]
    behind = [None] + [lax.rem(z + nz - d, nz) for d in (1, 2, 3)]
    lines = [None] + [(toward[d], c, k) for d in (1, 2, 3)]
    count = [0]
    local_count = [0]
    pending = []

    def send(src, dst, device):
        i = count[0]
        count[0] += 1
        copy = pltpu.make_async_remote_copy(
            src_ref=src, dst_ref=dst, send_sem=ssem.at[i], recv_sem=rsem.at[i],
            device_id=device, device_id_type=MESH,
        )
        copy.start()
        pending.append(copy)
        return copy

    def local(src, dst):
        i = local_count[0]
        local_count[0] += 1
        copy = pltpu.make_async_copy(src, dst, lsem.at[i])
        copy.start()
        return copy

    def flush(copies):
        for copy in copies:
            copy.wait_send()
            pending[:] = [other for other in pending if other is not copy]

    tok = x_ref.shape[0]
    half = tok // 2
    total = xf.shape[0]
    width = xf.shape[1]
    steps = total // SUB
    states = h.shape[1]
    wide = 2 * LANES
    block = w_s.shape[1] // 4
    tiles = (0, 1)
    rb = 128
    nblk = total // rb

    def lanes(t):
        return slice(t * LANES, (t + 1) * LANES)

    def blk(i):
        return pl.ds(pl.multiple_of(i * rb, rb), rb)

    def tau_rows(tau):
        return at8(tau * SUB, SUB)

    def loop(n, body, unroll=1):
        def step(i, carry):
            body(i)
            return carry

        lax.fori_loop(0, n, step, 0, unroll=unroll)

    barrier = pltpu.get_barrier_semaphore()
    everyone = [sib] + peers[1:] + [(z, plane[p], 1 - k) for p in (1, 2, 3)] + lines[1:]
    for device in everyone:
        pl.semaphore_signal(barrier, inc=1, device_id=device, device_id_type=MESH)
    chans = pl.ds(pl.multiple_of(c * wide, wide), wide)
    spart[...] = jnp.zeros_like(spart)
    spart[0, XP : XP + 24, :] = xproj_ref[:, chans].astype(F32)
    spart[0, DTW : DTW + 16, :] = dtw_ref[:, chans].astype(F32)
    spart[0, ALOG : ALOG + 4, :] = alog_ref[:, chans].astype(F32)
    spart[0, CONVW : CONVW + 4, :] = convw_ref[...].astype(F32)
    spart[0, CONVB : CONVB + 1, :] = convb_ref[...].astype(F32)
    spart[0, DTB : DTB + 1, :] = dtb_ref[...].astype(F32)
    spart[0, SKIP : SKIP + 1, :] = skip_ref[...].astype(F32)
    spart[0, GAIN : GAIN + 1, :] = gain_ref[...].astype(F32)
    pk_s[z] = spart[0].astype(BF16)
    segs[c] = jnp.broadcast_to(seg_ref[...], (SUB, tok))
    pl.semaphore_wait(barrier, len(everyone))

    s_pack = [send(pk_s.at[z], pk_s.at[z], lines[d]) for d in (1, 2, 3)]
    s_seg = [send(segs.at[c], segs.at[c], peers[p]) for p in (1, 2, 3)]
    my_half = pl.ds(pl.multiple_of(c * tok + k * half, half), half)
    s_x = [send(x_ref.at[pl.ds(pl.multiple_of(k * half, half), half)], xf.at[my_half], peers[p]) for p in (3, 1, 2)]

    zrows = pl.ds(pl.multiple_of(z * block, block), block)

    def weight(which):
        return [
            send(win_ref.at[which, :, chans], w_s.at[which, zrows, :], lines[d]) for d in (1, 2, 3)
        ]

    s_wx = weight(0)
    own_w = [local(win_ref.at[i, :, chans], w_s.at[i, zrows, :]) for i in (0, 1)]
    zcols = pl.ds(pl.multiple_of(z * block, block), block)
    own_wo = local(wout_ref.at[chans, :], wo_s.at[:, zcols])

    own_rows = pl.ds(pl.multiple_of(c * tok, tok), tok)
    xf[own_rows, :] = x_ref[...]
    mrow = mask_ref[...].astype(F32)
    for b in range(tok // LANES):
        rows = slice(b * LANES, (b + 1) * LANES)
        maskc[rows, :] = jnp.broadcast_to(mrow[:, rows], (LANES, LANES)).T
    mcol = jnp.concatenate([maskc[...]] * (width // LANES), axis=1)
    mg[own_rows, :] = (og_ref[...].astype(F32) * mcol).astype(BF16)

    def halves(copies, buf):
        relays = []
        for copy, p in zip(copies, (3, 1, 2)):
            copy.wait_recv()
            rows = pl.ds(pl.multiple_of(plane[p] * tok + k * half, half), half)
            relays.append(send(buf.at[rows], buf.at[rows], sib))
        return relays

    r_x = halves(s_x, xf)
    s_mg = [send(mg.at[my_half], mg.at[my_half], peers[p]) for p in (3, 1, 2)]

    for copy in s_pack:
        copy.wait_recv()
    for i in range(4):
        pk_f[i] = pk_s[i].astype(F32)
    for i in range(4):
        alg[4 * i : 4 * i + 4, :] = pk_f[i, ALOG : ALOG + 4, :]
    xp_rows = jnp.concatenate([pk_f[i, XP : XP + 24, :] for i in range(4)] + [jnp.zeros((32, wide), F32)], axis=0)
    xp[...] = xp_rows.astype(BF16)
    dt_rows = jnp.concatenate([pk_f[i, DTW : DTW + 16, :] for i in range(4)] + [jnp.zeros((64, wide), F32)], axis=0)
    dtwp[...] = dt_rows.astype(BF16)
    a2v = -jnp.exp(alg[...]) * LOG2E
    for n in range(states):
        for t in tiles:
            a2b[t, n] = jnp.broadcast_to(a2v[n : n + 1, lanes(t)], (SUB, LANES))
    gain_row = jnp.concatenate([pk_f[i, GAIN : GAIN + 1, :] for i in range(4)], axis=1)
    sown[...] = pk_f[c]

    def param(row, t):
        return sown[row : row + 1, lanes(t)]

    for copy in s_seg:
        copy.wait_recv()
    for i in range(4):
        srow = segs[i, 0:1, :].astype(F32)
        for b in range(tok // LANES):
            rows = slice(b * LANES, (b + 1) * LANES)
            nat[0, i * tok + b * LANES : i * tok + (b + 1) * LANES, :] = jnp.broadcast_to(
                srow[:, rows], (LANES, LANES)
            ).T

    def seg_in(tau):
        segp[at8(PAD + tau * SUB, SUB), :] = nat[0, pl.ds(tau, SUB, stride=steps), :]

    loop(steps, seg_in, 8)
    sub_row = lax.broadcasted_iota(jnp.int32, (SUB, LANES), 0)

    def from_before(v, fill):
        return jnp.where(sub_row >= 1, pltpu.roll(v, 1, 0), fill)

    def from_after(v, fill):
        return jnp.where(sub_row < SUB - 1, pltpu.roll(v, SUB - 1, 0), fill)

    for j in range(3):
        segp[j * SUB : (j + 1) * SUB, :] = from_before(segp[total + j * SUB : total + (j + 1) * SUB, :], -1.0)
        segp[PAD + total + j * SUB : PAD + total + (j + 1) * SUB, :] = from_after(
            segp[PAD + j * SUB : PAD + (j + 1) * SUB, :], -2.0
        )

    for copy in r_x:
        copy.wait_recv()

    def norm(i):
        v = xf[blk(i), :].astype(F32)
        r = lax.rsqrt(jnp.mean(v * v, axis=1, keepdims=True) + EPS)
        xf[blk(i), :] = (v * r * gain_row).astype(BF16)

    flush(s_x + r_x)
    loop(nblk, norm)

    def project(which, dst, off):
        def body(i):
            v = dot(xf[blk(i), :], w_s[which]).astype(BF16).astype(F32)
            for t in tiles:
                nat[t, blk(i), :] = v[:, lanes(t)]

        loop(nblk, body)
        permute_in(dst, off)

    def permute_in(dst, off):
        def body(tau):
            for t in tiles:
                dst[t, at8(off + tau * SUB, SUB), :] = nat[t, pl.ds(tau, SUB, stride=steps), :]

        loop(steps, body, 8)

    def permute_out(src, dst):
        def body(i):
            for s in range(SUB):
                for t in tiles:
                    nat[t, at8(s * steps + i * SUB, SUB), :] = src[t, pl.ds(i * SUB * SUB + s, SUB, stride=SUB), :]

        loop(steps // SUB, body)

        def cast(i):
            dst[blk(i), :] = jnp.concatenate([nat[t, blk(i), :] for t in tiles], axis=1).astype(BF16)

        loop(nblk, cast)

    for copy in s_wx:
        copy.wait_recv()
    own_w[0].wait()
    s_wz = weight(1)
    project(0, inner, PAD)
    for t in tiles:
        for j in range(3):
            inner[t, j * SUB : (j + 1) * SUB, :] = from_before(inner[t, total + j * SUB : total + (j + 1) * SUB, :], 0.0)

    def conv(i):
        for t in tiles:
            mine = segp[at8(PAD + i * rb, rb), :]
            pre = jnp.zeros((rb, LANES), F32) + param(CONVB, t)
            for j in range(4):
                window = inner[t, at8(PAD + i * rb - j * SUB, rb), :]
                if j:
                    window = jnp.where(segp[at8(PAD + i * rb - j * SUB, rb), :] == mine, window, 0.0)
                pre = pre + param(CONVW + 3 - j, t) * window
            s = jax.nn.sigmoid(pre)
            act[t, blk(i), :] = (pre * s).astype(BF16).astype(F32)
            slope[t, blk(i), :] = s * (1.0 + pre * (1.0 - s))

    loop(nblk, conv)

    def tiles_bf(ref, i):
        return jnp.concatenate([ref[t, blk(i), :] for t in tiles], axis=1).astype(BF16)

    def mix(i):
        mp[i] = dot_nt(tiles_bf(act, i), xp[...])

    loop(nblk, mix)

    def plane_sum(out, between):
        first = send(mp.at[pl.ds((1 - k) * 4, 4)], recv_a, sib)
        between[0]()
        first.wait_recv()
        for i in range(4):
            sum_a[i] = mp[k * 4 + i] + recv_a[i]
        second = [send(sum_a.at[plane[p]], recv_b.at[p - 1], peers[p]) for p in (3, 1, 2)]
        between[1]()
        for copy in second:
            copy.wait_recv()
        mine = k * 4 + c
        out[mine] = sum_a[c] + recv_b[0] + recv_b[1] + recv_b[2]
        third = [send(out.at[mine], out.at[mine], peers[p]) for p in (3, 1, 2)]
        third.append(send(out.at[mine], out.at[mine], sib))
        between[2]()
        fourth = []
        for copy, p in zip(third, (3, 1, 2)):
            copy.wait_recv()
            there = k * 4 + plane[p]
            fourth.append(send(out.at[there], out.at[there], sib))
        between[3]()
        for copy in [third[3]] + fourth:
            copy.wait_recv()
        flush([first] + second + third + fourth)

    late = {}
    mm = gnat

    def gates():
        for copy in s_wz:
            copy.wait_recv()
        own_w[1].wait()
        late["wo"] = [send(wout_ref.at[chans, :], wo_s.at[:, zcols], lines[d]) for d in (1, 2, 3)]
        project(1, gate, 0)

    def nothing():
        pass

    def relay_mg():
        late["mg"] = halves(s_mg, mg)

    plane_sum(full, [nothing, relay_mg, gates, nothing])

    def steps_of(i):
        arg = dot(full[i].astype(BF16), dtwp[...])
        for t in tiles:
            v = arg[:, lanes(t)] + param(DTB, t)
            dt[t, blk(i), :] = jnp.maximum(v, 0.0) + jnp.log1p(jnp.exp(-jnp.abs(v)))
        hi = full[i].astype(BF16)
        lo = (full[i] - hi.astype(F32)).astype(BF16)
        mm[blk(i), :] = jnp.concatenate([hi, lo], axis=1)

    loop(nblk, steps_of)

    def spread(g):
        row = lax.rem(lax.broadcasted_iota(jnp.int32, (wide, 4 * LANES), 0), LANES)
        col = lax.broadcasted_iota(jnp.int32, (wide, 4 * LANES), 1) // LANES
        pick = jnp.where(row == 64 + g * 4 + col, 1.0, 0.0).astype(BF16)
        for i in range(total // 256):
            v = dot(mm[i * 256 : (i + 1) * 256, :], pick)
            for q in range(4):
                bc[g * 4 + q, i * 256 : (i + 1) * 256, :] = v[:, lanes(q)]

    loop(2 * states // 4, spread)

    def dts(t, tau):
        v = dt[t, tau_rows(tau), :]
        r = at8(PAD + tau * SUB, SUB)
        p = at8(PAD + tau * SUB - SUB, SUB)
        return v, jnp.where(segp[r, :] == segp[p, :], v, KILL)

    for t in tiles:

        def ends(tau, carry, t=t):
            v, killed = dts(t, tau)
            drive = v * act[t, tau_rows(tau), :]
            new = [
                carry[n] * jnp.exp2(killed * a2b[t, n]) + drive * bc[n, tau_rows(tau), :] for n in range(states)
            ]
            return tuple(new) + (carry[states] + killed,)

        zero = jnp.zeros((SUB, LANES), F32)
        got = lax.fori_loop(0, steps, ends, (zero,) * (states + 1), unroll=4)
        cum[t] = got[states]
        for n in range(states):
            st[t, n] = prefix_of(got[n], jnp.exp2(got[states] * a2b[t, n]))

    for t in tiles:
        for n in range(states):
            h[t, n, 0:SUB, :] = st[t, n]

        def forward(tau, carry, t=t):
            v, killed = dts(t, tau)
            drive = v * act[t, tau_rows(tau), :]
            new, parts = [], [None] * 4
            for n in range(states):
                s = carry[n] * jnp.exp2(killed * a2b[t, n]) + drive * bc[n, tau_rows(tau), :]
                h[t, n, at8(tau * SUB + SUB, SUB), :] = s
                o = s * bc[states + n, tau_rows(tau), :]
                parts[n % 4] = o if parts[n % 4] is None else parts[n % 4] + o
                new.append(s)
            y[t, tau_rows(tau), :] = (parts[0] + parts[1]) + (parts[2] + parts[3])
            return tuple(new)

        lax.fori_loop(0, steps, forward, tuple(st[t, n] for n in range(states)), unroll=4)

    for copy in late["mg"] + late["wo"]:
        copy.wait_recv()
    own_wo.wait()

    def ograd(i):
        v = dot_nt(mg[blk(i), :], wo_s[...])
        for t in tiles:
            nat[t, blk(i), :] = v[:, lanes(t)]

    loop(nblk, ograd)
    gb = SUB * SUB

    def strided(t, i):
        return jnp.concatenate([nat[t, pl.ds(i * SUB + u, SUB, stride=steps), :] for u in range(SUB)], axis=0)

    def gating(i, carry):
        new = []
        rows = pl.ds(pl.multiple_of(i * gb, gb), gb)
        for t in tiles:
            gv, ov, av = gate[t, rows, :], strided(t, i), act[t, rows, :]
            s = jax.nn.sigmoid(gv)
            ytot = y[t, rows, :] + param(SKIP, t) * av
            gy = ov * (gv * s)
            yg[t, rows, :] = gy
            y[t, rows, :] = ytot * (gv * s)
            gate[t, rows, :] = ov * ytot * (s * (1.0 + gv * (1.0 - s)))
            new.append(carry[t] + jnp.sum((gy * av).reshape(SUB, SUB, LANES), axis=0))
        return tuple(new)

    zero = jnp.zeros((SUB, LANES), F32)
    skip_sum = lax.fori_loop(0, total // gb, gating, (zero, zero))
    permute_out(y, gnat)
    permute_out(gate, znat)

    def owner_rows(i, q):
        return pl.ds(pl.multiple_of(i * tok + q * half, half), half)

    def start_rows(partial):
        def other(i):
            big_send[i] = partial(owner_rows(i, 1 - k)).astype(BF16)

        loop(4, other)
        first = send(big_send, big_recv, sib)

        def mine(i):
            big_keep[i] = partial(owner_rows(i, k)).astype(BF16)

        loop(4, mine)
        return first

    def middle_rows(first):
        first.wait_recv()

        def add(i):
            big_keep[i] = (big_keep[i].astype(F32) + big_recv[i].astype(F32)).astype(BF16)

        loop(4, add)
        return [send(big_keep.at[plane[p]], big_rb.at[p - 1], peers[p]) for p in (3, 1, 2)]

    def end_rows(second):
        for copy in second:
            copy.wait_recv()
        v = big_keep[c].astype(F32)
        for p in range(3):
            v = v + big_rb[p].astype(F32)
        return v

    branch_a = start_rows(lambda r: dot(gnat[r, :], wo_s[...]))

    def weight_grad(slot, left, right):
        gpart[slot % 2] = dot_tn(left[...], right[...]).astype(BF16)
        return [
            send(
                gpart.at[slot % 2, :, pl.ds(pl.multiple_of(toward[d] * block, block), block)],
                zrecv.at[slot, d - 1],
                lines[d],
            )
            for d in (1, 2, 3)
        ]

    def owned_grad(slot, copies):
        for copy in copies:
            copy.wait_recv()
        v = gpart[slot % 2, :, zcols].astype(F32)
        for d in range(3):
            v = v + zrecv[slot, d].astype(F32)
        return v

    def share(slot, dst):
        return [local(gres.at[slot], dst)] + [send(gres.at[slot], dst, peers[p]) for p in (3, 1, 2)]

    z_wo = weight_grad(2, gnat, mg)
    z_wz = weight_grad(1, znat, xf)

    for t in tiles:

        def back_ends(i, carry, t=t):
            tau = steps - 1 - i
            _, killed = dts(t, tau)
            gy = yg[t, tau_rows(tau), :]
            return tuple(
                (carry[n] + gy * bc[states + n, tau_rows(tau), :]) * jnp.exp2(killed * a2b[t, n])
                for n in range(states)
            )

        got = lax.fori_loop(0, steps, back_ends, (zero,) * states, unroll=4)
        for n in range(states):
            gin[t, n] = suffix_of(got[n], jnp.exp2(cum[t] * a2b[t, n]))

    branch_b = middle_rows(branch_a)
    flush([branch_a])
    so_s = big_send.at[0]

    gsum, dsum = gate, y
    part = states // 2
    for lo in (0, part):
        names = list(range(lo, lo + part))

        def back(i, carry, names=names, lo=lo):
            grads, acc = carry
            tau = steps - 1 - i
            r = tau_rows(tau)
            pair = [dts(t, tau) for t in tiles]
            drive = [pair[t][0] * act[t, r, :] for t in tiles]
            gy = [yg[t, r, :] for t in tiles]
            along = [None, None]
            down = [None, None]
            new_g, new_a = [], []
            for q, n in enumerate(names):
                bv, cv = bc[n, r, :], bc[states + n, r, :]
                pb = pc = None
                for t in tiles:
                    a2 = a2b[t, n]
                    decay = jnp.exp2(pair[t][1] * a2)
                    g = grads[2 * q + t] + gy[t] * cv
                    gb = g * bv
                    along[t] = gb if along[t] is None else along[t] + gb
                    v = g * drive[t]
                    pb = v if pb is None else pb + v
                    v = gy[t] * h[t, n, at8(tau * SUB + SUB, SUB), :]
                    pc = v if pc is None else pc + v
                    gd = g * decay
                    dla = gd * h[t, n, r, :]
                    v = dla * a2
                    down[t] = v if down[t] is None else down[t] + v
                    new_a.append(acc[2 * q + t] + dla * pair[t][0])
                    new_g.append(gd)
                bc[n, r, :] = pb
                bc[states + n, r, :] = pc
            for t in tiles:
                if lo == 0:
                    gsum[t, r, :] = along[t]
                    dsum[t, r, :] = down[t]
                else:
                    gsum[t, r, :] = gsum[t, r, :] + along[t]
                    dsum[t, r, :] = dsum[t, r, :] + down[t]
            return tuple(new_g), tuple(new_a)

        start = tuple(gin[t, n] for n in names for t in tiles)
        _, acc = lax.fori_loop(0, steps, back, (start, (zero,) * (2 * part)), unroll=2)
        for q, n in enumerate(names):
            for t in tiles:
                alg[n : n + 1, lanes(t)] = (
                    jnp.sum(acc[2 * q + t], axis=0, keepdims=True) * a2b[t, n][0:1, :] * LN2
                )

    def lin(i, carry):
        new = []
        rank = []
        for t in tiles:
            av, gv = act[t, blk(i), :], gsum[t, blk(i), :]
            v = (dsum[t, blk(i), :] * LN2 + av * gv) * one_less_exp(dt[t, blk(i), :])
            new.append(carry[t] + jnp.sum(v.reshape(rb // SUB, SUB, LANES), axis=0))
            low = v.astype(BF16)
            rank.append(low)
            dsum[t, blk(i), :] = low.astype(F32)
            gsum[t, blk(i), :] = dt[t, blk(i), :] * gv + param(SKIP, t) * yg[t, blk(i), :]
        mp[i] = dot_nt(jnp.concatenate(rank, axis=1), dtwp[...])
        return tuple(new)

    dtb_sum = lax.fori_loop(0, nblk, lin, (zero, zero))

    def collect(i):
        v = mp[i]
        for n in range(0, 2 * states, 2):
            row = lax.broadcasted_iota(jnp.int32, (wide, LANES), 0) // LANES
            col = lax.broadcasted_iota(jnp.int32, (wide, LANES), 1)
            pick = jnp.where(col == 64 + n + row, 1.0, 0.0).astype(BF16)
            pair = jnp.concatenate([bc[n, blk(i), :], bc[n + 1, blk(i), :]], axis=1).astype(BF16)
            v = v + dot(pair, pick)
        mp[i] = v

    loop(nblk, collect)

    def finish_early():
        v = end_rows(branch_b)
        rows = pl.ds(pl.multiple_of(k * half, half), half)
        mk = jnp.concatenate([maskc[rows, :]] * (width // LANES), axis=1)
        so_s[...] = (x_ref[rows, :].astype(F32) + mk * v).astype(BF16)
        late["so"] = [local(so_s, so_out.at[rows, :]), send(so_s, so_out.at[rows, :], sib)]
        v = owned_grad(2, z_wo)
        gres[2] = v.astype(BF16)
        late["gwo"] = share(2, wo_out.at[chans, :])

    def finish_wz():
        v = owned_grad(1, z_wz).T
        gres[1] = v.astype(BF16)
        late["gwz"] = share(1, wg_out.at[1, :, chans])
        late["gain"] = v * w_s[1, zrows, :].astype(F32)

    def dtw_grad():
        low = jnp.concatenate([full[i].astype(BF16) for i in range(nblk)], axis=0)
        linv = jnp.concatenate([tiles_bf(dsum, i) for i in range(nblk)], axis=0)
        g = dot_tn(low, linv)
        for i in range(4):
            spart[i, DTW : DTW + 16, :] = g[i * 16 : i * 16 + 16, :]

    plane_sum(full2, [dtw_grad, finish_early, finish_wz, nothing])

    pg = slope

    def pre_grad(i, carry):
        mixg = full2[i].astype(BF16)
        back_x = dot(mixg, xp[...])
        new = []
        for t in tiles:
            v = (gsum[t, blk(i), :] + back_x[:, lanes(t)]) * pg[t, blk(i), :]
            pg[t, blk(i), :] = v
            mine = segp[at8(PAD + i * rb, rb), :]
            new.append(carry[5 * t] + jnp.sum(v.reshape(rb // SUB, SUB, LANES), axis=0))
            for j in range(4):
                window = inner[t, at8(PAD + i * rb - j * SUB, rb), :]
                if j:
                    window = jnp.where(segp[at8(PAD + i * rb - j * SUB, rb), :] == mine, window, 0.0)
                new.append(carry[5 * t + 1 + j] + jnp.sum((v * window).reshape(rb // SUB, SUB, LANES), axis=0))
        return tuple(new)

    conv_sum = lax.fori_loop(0, nblk, pre_grad, (zero,) * 10)
    for t in tiles:
        for j in range(3):
            pg[t, total + j * SUB : total + (j + 1) * SUB, :] = from_after(pg[t, j * SUB : (j + 1) * SUB, :], 0.0)

    def inner_grad(i):
        for t in tiles:
            mine = segp[at8(PAD + i * rb, rb), :]
            v = pg[t, blk(i), :] * param(CONVW + 3, t)
            for j in range(1, 4):
                later = pg[t, at8(i * rb + j * SUB, rb), :]
                same = segp[at8(PAD + i * rb + j * SUB, rb), :] == mine
                v = v + jnp.where(same, later, 0.0) * param(CONVW + 3 - j, t)
            dsum[t, blk(i), :] = v

    loop(nblk, inner_grad)
    permute_out(dsum, gnat)
    flush(z_wo)
    z_wx = weight_grad(0, gnat, xf)

    flush(late["so"][1:] + branch_b)
    late["so"][0].wait()
    norm_a = start_rows(lambda r: dot_nt(gnat[r, :], w_s[0]) + dot_nt(znat[r, :], w_s[1]))

    mixv = jnp.concatenate([full2[i].astype(BF16) for i in range(nblk)], axis=0)
    actv = jnp.concatenate([tiles_bf(act, i) for i in range(nblk)], axis=0)
    gx = dot_tn(mixv, actv)
    for i in range(4):
        spart[i, XP : XP + 24, :] = gx[i * 24 : i * 24 + 24, :]
        spart[i, ALOG : ALOG + 4, :] = alg[i * 4 : i * 4 + 4, :]
        for t in tiles:
            for j in range(4):
                spart[i, CONVW + 3 - j : CONVW + 4 - j, lanes(t)] = jnp.sum(
                    conv_sum[5 * t + 1 + j], axis=0, keepdims=True
                )
            spart[i, CONVB : CONVB + 1, lanes(t)] = jnp.sum(conv_sum[5 * t], axis=0, keepdims=True)
            spart[i, DTB : DTB + 1, lanes(t)] = jnp.sum(dtb_sum[t], axis=0, keepdims=True)
            spart[i, SKIP : SKIP + 1, lanes(t)] = jnp.sum(skip_sum[t], axis=0, keepdims=True)
    z_small = [send(spart.at[toward[d]], srecv.at[d - 1], lines[d]) for d in (1, 2, 3)]

    norm_b = middle_rows(norm_a)

    for copy in z_small:
        copy.wait_recv()
    sfull[c] = spart[z] + srecv[0] + srecv[1] + srecv[2]
    g_small = [send(sfull.at[c], sfull.at[c], peers[p]) for p in (3, 1, 2)]

    v = owned_grad(0, z_wx).T
    gres[0] = v.astype(BF16)
    late["gwx"] = share(0, wg_out.at[0, :, chans])
    v = late["gain"] + v * w_s[0, zrows, :].astype(F32)
    v = v[:, :LANES] + v[:, LANES:]
    for b in range(block // LANES):
        col = v[b * LANES : (b + 1) * LANES, :].T
        ggs[0, :, lanes(b)] = jnp.broadcast_to(jnp.sum(col, axis=0, keepdims=True), (SUB, LANES))
    s_gain = [send(ggs.at[0], ggs.at[p], peers[p]) for p in (1, 2, 3)]
    s_gain += [send(ggs.at[0], ggs.at[3 + p], (z, plane[p], 1 - k)) for p in (1, 2, 3)]
    s_gain.append(send(ggs.at[0], ggs.at[7], sib))

    ng = end_rows(norm_b)
    rows = pl.ds(pl.multiple_of(k * half, half), half)
    xv = x_ref[rows, :].astype(F32)
    r = lax.rsqrt(jnp.mean(xv * xv, axis=1, keepdims=True) + EPS)
    sg = ng * gain_row
    sg_s[...] = (
        og_ref[rows, :].astype(F32) + r * sg - xv * (r * r * r) * jnp.mean(sg * xv, axis=1, keepdims=True)
    )
    last = [local(sg_s, sg_out.at[rows, :]), send(sg_s, sg_out.at[rows, :], sib)]

    for copy in g_small:
        copy.wait_recv()
    for i in range(4):
        sm_out[:, i * wide : (i + 1) * wide] = sfull[i]
    cv_out[...] = sfull[z, CONVW : CONVW + 8, :]
    for copy in s_gain:
        copy.wait_recv()
    v = ggs[0]
    for i in range(1, 8):
        v = v + ggs[i]
    gg_out[...] = v[0:1, :] / gain_ref[...].astype(F32)

    late["so"][1].wait_recv()
    for name in ("gwo", "gwz", "gwx"):
        late[name][0].wait()
        for copy in late[name][1:]:
            copy.wait_recv()
    last[0].wait()
    last[1].wait_recv()
    flush(list(pending))


def fused(
    stream_in, norm_gain, in_weight, out_weight, xproj_weight, dt_weight, a_log, convolution_weight,
    convolution_bias, step_size_bias, skip_term_scale, seg_ids, pad_mask, out_grad,
):
    _, tok, width = stream_in.shape
    wide = 2 * LANES
    total = 4 * tok
    block = width // 4
    states = 4 * a_log.shape[0]
    vm = pl.BlockSpec(memory_space=pltpu.VMEM)
    hbm = pl.BlockSpec(memory_space=pl.ANY)
    f, b = (lambda *s: pltpu.VMEM(s, F32)), (lambda *s: pltpu.VMEM(s, BF16))
    scan = f(2, total, LANES)
    scratch = dict(
        xf=b(total, width), mg=b(total, width), w_s=b(2, width, wide), wo_s=b(wide, width),
        pk_f=f(4, ROWS, wide), pk_s=b(4, ROWS, wide), segs=pltpu.VMEM((4, SUB, tok), jnp.int32),
        segp=f(total + 2 * PAD, LANES), maskc=f(tok, LANES), nat=scan, inner=f(2, total + PAD, LANES),
        slope=f(2, total + PAD, LANES), act=scan, gate=scan, dt=scan, yg=scan, y=scan,
        bc=f(2 * states, total, LANES), h=f(2, states, total + SUB, LANES), a2b=f(2, states, SUB, LANES),
        st=f(2, states, SUB, LANES), gin=f(2, states, SUB, LANES), cum=f(2, SUB, LANES), alg=f(states, wide),
        full=f(8, 128, LANES), full2=f(8, 128, LANES), mp=f(8, 128, LANES), sum_a=f(4, 128, LANES),
        recv_a=f(4, 128, LANES), recv_b=f(3, 128, LANES), xp=b(LANES, wide), dtwp=b(LANES, wide),
        big_send=b(4, tok // 2, width), big_keep=b(4, tok // 2, width),
        big_recv=b(4, tok // 2, width), big_rb=b(3, tok // 2, width), gpart=b(2, wide, width),
        zrecv=b(3, 3, wide, block), gres=b(3, block, wide), gnat=b(total, wide), znat=b(total, wide),
        spart=f(4, ROWS, wide), srecv=f(3, ROWS, wide), sfull=f(4, ROWS, wide), sown=f(ROWS, wide),
        ggs=f(8, SUB, block), sg_s=f(tok // 2, width),
        ssem=pltpu.SemaphoreType.DMA((112,)), rsem=pltpu.SemaphoreType.DMA((112,)),
        lsem=pltpu.SemaphoreType.DMA((12,)),
    )
    outs = pl.pallas_call(
        fused_kernel,
        out_shape=[
            jax.ShapeDtypeStruct((tok, width), BF16),
            jax.ShapeDtypeStruct((tok, width), F32),
            jax.ShapeDtypeStruct((2, block, 4 * wide), BF16),
            jax.ShapeDtypeStruct((4 * wide, block), BF16),
            jax.ShapeDtypeStruct((ROWS, 4 * wide), F32),
            jax.ShapeDtypeStruct((8, wide), F32),
            jax.ShapeDtypeStruct((1, block), F32),
        ],
        in_specs=[vm, vm, hbm, hbm] + [vm] * 10,
        out_specs=[hbm] * 4 + [vm] * 3,
        scratch_shapes=list(scratch.values()),
        compiler_params=pltpu.CompilerParams(
            collective_id=0, has_side_effects=True, vmem_limit_bytes=VMEM_LIMIT
        ),
    )(
        stream_in.reshape(tok, width), out_grad.reshape(tok, width), in_weight, out_weight, xproj_weight,
        dt_weight, a_log, convolution_weight.reshape(4, block), convolution_bias, step_size_bias,
        skip_term_scale, norm_gain.reshape(1, block), seg_ids, pad_mask,
    )
    so, sg, wg, wo, sm, cv, gg = outs
    return (
        so.reshape(1, tok, width),
        sg.reshape(1, tok, width),
        gg.reshape(block),
        wg.astype(F32),
        wo.astype(F32),
        sm[XP : XP + 24],
        sm[DTW : DTW + 16],
        sm[ALOG : ALOG + 4],
        cv[0:4].reshape(4, 1, wide),
        cv[4:5],
        cv[5:6],
        cv[6:7],
    )


def solution(mesh):
    in_specs = (
        P("dp", "ctx", None),
        P("dp"),
        P(None, "dp", "tp"),
        P("tp", "dp"),
        P("dp", "tp"),
        P("dp", "tp"),
        P("dp", "tp"),
        P(None, "tp", "dp"),
        P("tp", "dp"),
        P("tp", "dp"),
        P("tp", "dp"),
        P("dp", "ctx"),
        P("dp", "ctx"),
        P("dp", "ctx", None),
    )
    out_specs = (
        P("dp", "ctx", None),
        P("dp", "ctx", None),
        P("dp"),
        P(None, "dp", "tp"),
        P("tp", "dp"),
        P("dp", "tp"),
        P("dp", "tp"),
        P("dp", "tp"),
        P(None, "tp", "dp"),
        P("tp", "dp"),
        P("tp", "dp"),
        P("tp", "dp"),
    )

    def run(*args):
        stream, weight = args[0].shape, args[2].shape
        plane_fits = (mesh.shape["dp"], mesh.shape["ctx"], mesh.shape["tp"]) == (4, 4, 2)
        sizes_fit = stream == (4, 1024, 1024) and weight == (2, 1024, 2048)
        part = fused if plane_fits and sizes_fit else shards
        return jax.shard_map(
            part, mesh=mesh, in_specs=in_specs, out_specs=out_specs, check_vma=False
        )(*args)

    return run
```

profile of v0, /device:TPU:25, one launch (start us, length us, event | category | flops | bytes accessed | tf_op | source)
XLA Modules:
  0.0 145.8 jit_solution(15858283533351626207)
XLA Ops:
  0.6 1.2 reshape.51.gain_ref
  1.9 134.5 %shard_map.229 = (bf16[256,1024]{1,0:T(8,128)(2,1)}, f32[256,1024]{1,0:T(8,128)}, bf16[2,256,1024]{2,1,0:T(8,128)(2,1)}, bf16[1024,256]{1,0:T(8,128)(2,1)}, f32[...) custom-call(bf16[256,1024]{1,0:T(8,128)(2,1)} %bitcast.10, bf16[256,1024]{1,0:T(8,128)(2,1)} %bitcast.11, ...), custom_call_target="tpu_custom_call" | custom-call | tf_op jit(solution)/shard_map/pallas_call | solution.py:1185
  136.4 0.0 copy-start.1
  136.4 0.0 copy-start.3
  136.4 0.0 copy-start.4
  136.4 0.0 copy-start.2
  136.4 2.9 %convert_element_type.6 = f32[2,256,1024]{2,1,0:T(8,128)} convert(bf16[2,256,1024]{2,1,0:T(8,128)(2,1)} %get-tuple-element.22) | non-fusion elementwise | flops 524288 | bytes 3145728 | tf_op jit(solution)/shard_map/convert_element_type | solution.py:1212
  139.3 0.0 copy-start
  139.3 0.0 copy-done.1
  139.3 1.0 convert_element_type.7
  140.4 0.0 copy-start.5
  140.4 0.0 copy-done.3
  140.4 0.6 slice.21
  141.0 0.6 slice.22
  141.6 0.6 slice.23
  142.2 0.0 copy-done.4
  142.3 0.6 copy.26
  142.9 0.6 fusion
  143.4 0.0 copy-done.2
  143.4 0.8 copy.30
  144.2 0.0 copy-done
  144.2 1.0 copy.31
  145.2 0.0 copy-done.5
  145.2 0.6 copy.32
  (1 shorter events, 0.0 us)
Async XLA Ops:
  136.4 2.9 %copy-start.1 = (bf16[1024,256]{1,0:T(8,128)(2,1)S(1)}, bf16[1024,256]{1,0:T(8,128)(2,1)}, u32[]{:S(2)}) copy-start(bf16[1024,256]{1,0:T(8,128)(2,1)} %get-tuple-element.23) | copy-start | bytes 1572868
  136.4 4.0 %copy-start.3 = (f32[64,1024]{1,0:T(8,128)S(1)}, f32[64,1024]{1,0:T(8,128)}, u32[]{:S(2)}) copy-start(f32[64,1024]{1,0:T(8,128)} %get-tuple-element.24) | copy-start | bytes 786436
  136.4 5.9 %copy-start.4 = (f32[8,256]{1,0:T(8,128)S(1)}, f32[8,256]{1,0:T(8,128)}, u32[]{:S(2)}) copy-start(f32[8,256]{1,0:T(8,128)} %get-tuple-element.25) | copy-start | bytes 24580
  136.4 7.0 %copy-start.2 = (bf16[256,1024]{1,0:T(8,128)(2,1)S(1)}, bf16[256,1024]{1,0:T(8,128)(2,1)}, u32[]{:S(2)}) copy-start(bf16[256,1024]{1,0:T(8,128)(2,1)} %get-tuple-element.19) | copy-start | bytes 1572868
  139.3 4.9 %copy-start = (f32[256,1024]{1,0:T(8,128)S(1)}, f32[256,1024]{1,0:T(8,128)}, u32[]{:S(2)}) copy-start(f32[256,1024]{1,0:T(8,128)} %get-tuple-element.20) | copy-start | bytes 3145732
  140.4 4.8 %copy-start.5 = (f32[1,256]{1,0:T(1,128)S(1)}, f32[1,256]{1,0:T(1,128)}, u32[]{:S(2)}) copy-start(f32[1,256]{1,0:T(1,128)} %get-tuple-element.21) | copy-start | bytes 3076
where the time goes:
time: 147 us; the launch traced here: 146 us
  Pallas kernels  135 us (92%)
  local copies, waits for them, and re-layouts  6.63 us (5%)
  other arithmetic  3.93 us (3%)
    pallas_call x1, Pallas kernels, fused(): pl.pallas_call(fused_kernel, out_shape=[jax.ShapeDtypeStruct((tok, width)...  135 us
    unnamed x16, local copies, waits for them, and re-layouts  2.95 us

commit v1 on v0

--- a/solution.py
+++ b/solution.py
@@ -427,6 +427,8 @@
 PAD = 24
 ROWS = 64
 XP, DTW, ALOG, CONVW, CONVB, DTB, SKIP, GAIN = 0, 24, 40, 44, 48, 49, 50, 51
+A_DTW, A_ALOG, A_DTB, A_SKIP, A_ROWS = 0, 16, 20, 21, 24
+B_XP, B_CONVW, B_CONVB, B_ROWS = 0, 24, 28, 32
 NT = (((1,), (1,)), ((), ()))
 TN = (((0,), (0,)), ((), ()))
 
@@ -445,6 +447,15 @@
 
 def at8(start, size):
     return pl.ds(pl.multiple_of(start, 8), size)
+
+
+def sigmoid(v):
+    return 0.5 + 0.5 * jnp.tanh(0.5 * v)
+
+
+def log_one_plus(v):
+    series = v * (1.0 - v * (0.5 - v * (1.0 / 3.0 - v * 0.25)))
+    return jnp.where(v < 0.01, series, jnp.log(1.0 + v))
 
 
 def one_less_exp(v):
@@ -474,9 +485,9 @@
     x_ref, og_ref, win_ref, wout_ref, xproj_ref, dtw_ref, alog_ref, convw_ref, convb_ref, dtb_ref,
     skip_ref, gain_ref, seg_ref, mask_ref,
     so_out, sg_out, wg_out, wo_out, sm_out, cv_out, gg_out,
-    xf, mg, w_s, wo_s, pk_f, pk_s, segs, segp, maskc, nat, inner, slope, act, gate, dt, yg, y,
+    x_half, og_half, xf, mg, w_s, wo_s, pk_f, pk_s, segs, segp, maskc, nat, inner, slope, act, gate, dt, yg, y,
     bc, h, a2b, st, gin, cum, alg, full, full2, mp, sum_a, recv_a, recv_b, xp, dtwp,
-    big_send, big_keep, big_recv, big_rb, gpart, zrecv, gres, gnat, znat, spart, srecv, sfull, sown, ggs,
+    big_send, big_keep, big_recv, big_rb, gpart, zrecv, gres, gnat, znat, spart, srecv, sfull, bpart, brecv, bfull, sown, ggs,
     sg_s, ssem, rsem, lsem,
 ):
     z, c, k = lax.axis_index("dp"), lax.axis_index("ctx"), lax.axis_index("tp")
@@ -515,7 +526,7 @@
             copy.wait_send()
             pending[:] = [other for other in pending if other is not copy]
 
-    tok = x_ref.shape[0]
+    tok = maskc.shape[0]
     half = tok // 2
     total = xf.shape[0]
     width = xf.shape[1]
@@ -532,6 +543,11 @@
 
     def blk(i):
         return pl.ds(pl.multiple_of(i * rb, rb), rb)
+
+    wb = 512
+
+    def wide_blk(i):
+        return pl.ds(pl.multiple_of(i * wb, wb), wb)
 
     def tau_rows(tau):
         return at8(tau * SUB, SUB)
@@ -556,7 +572,7 @@
     spart[0, CONVB : CONVB + 1, :] = convb_ref[...].astype(F32)
     spart[0, DTB : DTB + 1, :] = dtb_ref[...].astype(F32)
     spart[0, SKIP : SKIP + 1, :] = skip_ref[...].astype(F32)
-    spart[0, GAIN : GAIN + 1, :] = gain_ref[...].astype(F32)
+    spart[0, GAIN : GAIN + 1, :] = gain_ref[...].astype(F32).reshape(1, block)
     pk_s[z] = spart[0].astype(BF16)
     segs[c] = jnp.broadcast_to(seg_ref[...], (SUB, tok))
     pl.semaphore_wait(barrier, len(everyone))
@@ -579,24 +595,17 @@
     own_wo = local(wout_ref.at[chans, :], wo_s.at[:, zcols])
 
     own_rows = pl.ds(pl.multiple_of(c * tok, tok), tok)
-    xf[own_rows, :] = x_ref[...]
+    half_rows = pl.ds(pl.multiple_of(k * half, half), half)
+    own_x = local(x_ref, xf.at[own_rows, :])
+    own_og = local(og_ref, mg.at[own_rows, :])
+    own_half = [local(x_ref.at[half_rows, :], x_half), local(og_ref.at[half_rows, :], og_half)]
     mrow = mask_ref[...].astype(F32)
     for b in range(tok // LANES):
         rows = slice(b * LANES, (b + 1) * LANES)
         maskc[rows, :] = jnp.broadcast_to(mrow[:, rows], (LANES, LANES)).T
     mcol = jnp.concatenate([maskc[...]] * (width // LANES), axis=1)
-    mg[own_rows, :] = (og_ref[...].astype(F32) * mcol).astype(BF16)
-
-    def halves(copies, buf):
-        relays = []
-        for copy, p in zip(copies, (3, 1, 2)):
-            copy.wait_recv()
-            rows = pl.ds(pl.multiple_of(plane[p] * tok + k * half, half), half)
-            relays.append(send(buf.at[rows], buf.at[rows], sib))
-        return relays
-
-    r_x = halves(s_x, xf)
-    s_mg = [send(mg.at[my_half], mg.at[my_half], peers[p]) for p in (3, 1, 2)]
+    own_og.wait()
+    mg[own_rows, :] = (mg[own_rows, :].astype(F32) * mcol).astype(BF16)
 
     for copy in s_pack:
         copy.wait_recv()
@@ -646,6 +655,17 @@
             segp[PAD + j * SUB : PAD + (j + 1) * SUB, :], -2.0
         )
 
+    def halves(copies, buf):
+        relays = []
+        for copy, p in zip(copies, (3, 1, 2)):
+            copy.wait_recv()
+            rows = pl.ds(pl.multiple_of(plane[p] * tok + k * half, half), half)
+            relays.append(send(buf.at[rows], buf.at[rows], sib))
+        return relays
+
+    r_x = halves(s_x, xf)
+    own_x.wait()
+
     for copy in r_x:
         copy.wait_recv()
 
@@ -654,16 +674,16 @@
         r = lax.rsqrt(jnp.mean(v * v, axis=1, keepdims=True) + EPS)
         xf[blk(i), :] = (v * r * gain_row).astype(BF16)
 
-    flush(s_x + r_x)
+    flush(r_x)
     loop(nblk, norm)
 
     def project(which, dst, off):
         def body(i):
-            v = dot(xf[blk(i), :], w_s[which]).astype(BF16).astype(F32)
+            v = dot(xf[wide_blk(i), :], w_s[which]).astype(BF16).astype(F32)
             for t in tiles:
-                nat[t, blk(i), :] = v[:, lanes(t)]
-
-        loop(nblk, body)
+                nat[t, wide_blk(i), :] = v[:, lanes(t)]
+
+        loop(total // wb, body)
         permute_in(dst, off)
 
     def permute_in(dst, off):
@@ -704,7 +724,7 @@
                 if j:
                     window = jnp.where(segp[at8(PAD + i * rb - j * SUB, rb), :] == mine, window, 0.0)
                 pre = pre + param(CONVW + 3 - j, t) * window
-            s = jax.nn.sigmoid(pre)
+            s = sigmoid(pre)
             act[t, blk(i), :] = (pre * s).astype(BF16).astype(F32)
             slope[t, blk(i), :] = s * (1.0 + pre * (1.0 - s))
 
@@ -723,13 +743,16 @@
         between[0]()
         first.wait_recv()
         for i in range(4):
-            sum_a[i] = mp[k * 4 + i] + recv_a[i]
+            sum_a[i] = (mp[k * 4 + i] + recv_a[i]).astype(BF16)
         second = [send(sum_a.at[plane[p]], recv_b.at[p - 1], peers[p]) for p in (3, 1, 2)]
         between[1]()
         for copy in second:
             copy.wait_recv()
         mine = k * 4 + c
-        out[mine] = sum_a[c] + recv_b[0] + recv_b[1] + recv_b[2]
+        v = mp[mine] + recv_a[c]
+        for p in range(3):
+            v = v + recv_b[p].astype(F32)
+        out[mine] = v.astype(BF16)
         third = [send(out.at[mine], out.at[mine], peers[p]) for p in (3, 1, 2)]
         third.append(send(out.at[mine], out.at[mine], sib))
         between[2]()
@@ -741,45 +764,48 @@
         between[3]()
         for copy in [third[3]] + fourth:
             copy.wait_recv()
-        flush([first] + second + third + fourth)
+        return [first] + second
 
     late = {}
-    mm = gnat
+
+    def send_wo():
+        late["wo"] = [send(wout_ref.at[chans, :], wo_s.at[:, zcols], lines[d]) for d in (1, 2, 3)]
 
     def gates():
         for copy in s_wz:
             copy.wait_recv()
         own_w[1].wait()
-        late["wo"] = [send(wout_ref.at[chans, :], wo_s.at[:, zcols], lines[d]) for d in (1, 2, 3)]
         project(1, gate, 0)
 
     def nothing():
         pass
 
-    def relay_mg():
-        late["mg"] = halves(s_mg, mg)
-
-    plane_sum(full, [nothing, relay_mg, gates, nothing])
+    def send_mg():
+        late["mg"] = [send(mg.at[my_half], mg.at[my_half], peers[p]) for p in (3, 1, 2)]
+
+    def gap():
+        send_mg()
+        gates()
+
+    first_sum = plane_sum(full, [nothing, nothing, send_wo, gap])
 
     def steps_of(i):
-        arg = dot(full[i].astype(BF16), dtwp[...])
+        arg = dot(full[i], dtwp[...])
         for t in tiles:
             v = arg[:, lanes(t)] + param(DTB, t)
-            dt[t, blk(i), :] = jnp.maximum(v, 0.0) + jnp.log1p(jnp.exp(-jnp.abs(v)))
-        hi = full[i].astype(BF16)
-        lo = (full[i] - hi.astype(F32)).astype(BF16)
-        mm[blk(i), :] = jnp.concatenate([hi, lo], axis=1)
+            dt[t, blk(i), :] = jnp.maximum(v, 0.0) + log_one_plus(jnp.exp(-jnp.abs(v)))
 
     loop(nblk, steps_of)
 
+    ahead = lax.broadcasted_iota(jnp.int32, (LANES, 4 * LANES), 0) - 64
+    ahead = ahead - lax.broadcasted_iota(jnp.int32, (LANES, 4 * LANES), 1) // LANES
+
     def spread(g):
-        row = lax.rem(lax.broadcasted_iota(jnp.int32, (wide, 4 * LANES), 0), LANES)
-        col = lax.broadcasted_iota(jnp.int32, (wide, 4 * LANES), 1) // LANES
-        pick = jnp.where(row == 64 + g * 4 + col, 1.0, 0.0).astype(BF16)
-        for i in range(total // 256):
-            v = dot(mm[i * 256 : (i + 1) * 256, :], pick)
+        pick = jnp.where(ahead == g * 4, 1.0, 0.0).astype(BF16)
+        for i in range(nblk // 2):
+            v = dot(jnp.concatenate([full[2 * i], full[2 * i + 1]], axis=0), pick)
             for q in range(4):
-                bc[g * 4 + q, i * 256 : (i + 1) * 256, :] = v[:, lanes(q)]
+                bc[g * 4 + q, i * 2 * rb : (i + 1) * 2 * rb, :] = v[:, lanes(q)]
 
     loop(2 * states // 4, spread)
 
@@ -806,6 +832,8 @@
             st[t, n] = prefix_of(got[n], jnp.exp2(got[states] * a2b[t, n]))
 
     for t in tiles:
+        if t:
+            late["mg"] = halves(late["mg"], mg)
         for n in range(states):
             h[t, n, 0:SUB, :] = st[t, n]
 
@@ -829,11 +857,11 @@
     own_wo.wait()
 
     def ograd(i):
-        v = dot_nt(mg[blk(i), :], wo_s[...])
+        v = dot_nt(mg[wide_blk(i), :], wo_s[...])
         for t in tiles:
-            nat[t, blk(i), :] = v[:, lanes(t)]
-
-    loop(nblk, ograd)
+            nat[t, wide_blk(i), :] = v[:, lanes(t)]
+
+    loop(total // wb, ograd)
     gb = SUB * SUB
 
     def strided(t, i):
@@ -844,7 +872,7 @@
         rows = pl.ds(pl.multiple_of(i * gb, gb), gb)
         for t in tiles:
             gv, ov, av = gate[t, rows, :], strided(t, i), act[t, rows, :]
-            s = jax.nn.sigmoid(gv)
+            s = sigmoid(gv)
             ytot = y[t, rows, :] + param(SKIP, t) * av
             gy = ov * (gv * s)
             yg[t, rows, :] = gy
@@ -861,37 +889,47 @@
     def owner_rows(i, q):
         return pl.ds(pl.multiple_of(i * tok + q * half, half), half)
 
-    def start_rows(partial):
-        def other(i):
-            big_send[i] = partial(owner_rows(i, 1 - k)).astype(BF16)
-
-        loop(4, other)
-        first = send(big_send, big_recv, sib)
-
-        def mine(i):
-            big_keep[i] = partial(owner_rows(i, k)).astype(BF16)
-
-        loop(4, mine)
+    pieces = ((3, 1, 2, 0),)
+
+    def start_rows(lefts, right):
+        def fill(dst, group, q):
+            there = [plane[p] if p else c for p in group]
+            rows = [jnp.concatenate([left[owner_rows(i, q), :] for i in there], axis=0) for left in lefts]
+
+            def body(j):
+                cols = pl.ds(pl.multiple_of(j * wide, wide), wide)
+                v = right(rows, cols)
+                for i, p in enumerate(group):
+                    dst[p, :, cols] = v[i * half : (i + 1) * half, :].astype(BF16)
+
+            loop(width // wide, body)
+
+        first = []
+        for group in pieces:
+            fill(big_send, group, 1 - k)
+            first += [send(big_send.at[p], big_recv.at[p], sib) for p in group]
+        for group in pieces:
+            fill(big_keep, group, k)
         return first
 
     def middle_rows(first):
-        first.wait_recv()
-
-        def add(i):
-            big_keep[i] = (big_keep[i].astype(F32) + big_recv[i].astype(F32)).astype(BF16)
-
-        loop(4, add)
-        return [send(big_keep.at[plane[p]], big_rb.at[p - 1], peers[p]) for p in (3, 1, 2)]
+        second = []
+        for copy, p in zip(first, pieces[0]):
+            copy.wait_recv()
+            big_keep[p] = (big_keep[p].astype(F32) + big_recv[p].astype(F32)).astype(BF16)
+            if p:
+                second.append(send(big_keep.at[p], big_rb.at[p - 1], peers[p]))
+        return second
 
     def end_rows(second):
         for copy in second:
             copy.wait_recv()
-        v = big_keep[c].astype(F32)
+        v = big_keep[0].astype(F32)
         for p in range(3):
             v = v + big_rb[p].astype(F32)
         return v
 
-    branch_a = start_rows(lambda r: dot(gnat[r, :], wo_s[...]))
+    branch_a = start_rows([gnat], lambda rows, cols: dot(rows[0], wo_s[:, cols]))
 
     def weight_grad(slot, left, right):
         gpart[slot % 2] = dot_tn(left[...], right[...]).astype(BF16)
@@ -919,6 +957,8 @@
     z_wz = weight_grad(1, znat, xf)
 
     for t in tiles:
+        if t:
+            branch_b = middle_rows(branch_a)
 
         def back_ends(i, carry, t=t):
             tau = steps - 1 - i
@@ -933,8 +973,7 @@
         for n in range(states):
             gin[t, n] = suffix_of(got[n], jnp.exp2(cum[t] * a2b[t, n]))
 
-    branch_b = middle_rows(branch_a)
-    flush([branch_a])
+    flush(branch_a)
     so_s = big_send.at[0]
 
     gsum, dsum = gate, y
@@ -990,6 +1029,9 @@
                     jnp.sum(acc[2 * q + t], axis=0, keepdims=True) * a2b[t, n][0:1, :] * LN2
                 )
 
+    gres[2] = owned_grad(2, z_wo).astype(BF16)
+    late["gwo"] = share(2, wo_out.at[chans, :])
+
     def lin(i, carry):
         new = []
         rank = []
@@ -1004,49 +1046,64 @@
         mp[i] = dot_nt(jnp.concatenate(rank, axis=1), dtwp[...])
         return tuple(new)
 
+    flush(first_sum)
     dtb_sum = lax.fori_loop(0, nblk, lin, (zero, zero))
 
+    beside = lax.broadcasted_iota(jnp.int32, (wide, LANES), 1) - 64
+    beside = beside - lax.broadcasted_iota(jnp.int32, (wide, LANES), 0) // LANES
+
     def collect(i):
-        v = mp[i]
+        rows = pl.ds(pl.multiple_of(i * 2 * rb, 2 * rb), 2 * rb)
+        v = jnp.concatenate([mp[2 * i], mp[2 * i + 1]], axis=0)
         for n in range(0, 2 * states, 2):
-            row = lax.broadcasted_iota(jnp.int32, (wide, LANES), 0) // LANES
-            col = lax.broadcasted_iota(jnp.int32, (wide, LANES), 1)
-            pick = jnp.where(col == 64 + n + row, 1.0, 0.0).astype(BF16)
-            pair = jnp.concatenate([bc[n, blk(i), :], bc[n + 1, blk(i), :]], axis=1).astype(BF16)
+            pick = jnp.where(beside == n, 1.0, 0.0).astype(BF16)
+            pair = jnp.concatenate([bc[n, rows, :], bc[n + 1, rows, :]], axis=1).astype(BF16)
             v = v + dot(pair, pick)
-        mp[i] = v
-
-    loop(nblk, collect)
+        mp[2 * i] = v[:rb, :]
+        mp[2 * i + 1] = v[rb:, :]
+
+    loop(nblk // 2, collect)
 
     def finish_early():
         v = end_rows(branch_b)
-        rows = pl.ds(pl.multiple_of(k * half, half), half)
-        mk = jnp.concatenate([maskc[rows, :]] * (width // LANES), axis=1)
-        so_s[...] = (x_ref[rows, :].astype(F32) + mk * v).astype(BF16)
-        late["so"] = [local(so_s, so_out.at[rows, :]), send(so_s, so_out.at[rows, :], sib)]
-        v = owned_grad(2, z_wo)
-        gres[2] = v.astype(BF16)
-        late["gwo"] = share(2, wo_out.at[chans, :])
-
-    def finish_wz():
+        mk = jnp.concatenate([maskc[half_rows, :]] * (width // LANES), axis=1)
+        for copy in own_half:
+            copy.wait()
+        so_s[...] = (x_half[...].astype(F32) + mk * v).astype(BF16)
+        late["so"] = [local(so_s, so_out.at[half_rows, :]), send(so_s, so_out.at[half_rows, :], sib)]
+
+    def finish_z():
         v = owned_grad(1, z_wz).T
         gres[1] = v.astype(BF16)
-        late["gwz"] = share(1, wg_out.at[1, :, chans])
         late["gain"] = v * w_s[1, zrows, :].astype(F32)
 
-    def dtw_grad():
-        low = jnp.concatenate([full[i].astype(BF16) for i in range(nblk)], axis=0)
+    def small_a():
+        low = jnp.concatenate([full[i] for i in range(nblk)], axis=0)
         linv = jnp.concatenate([tiles_bf(dsum, i) for i in range(nblk)], axis=0)
         g = dot_tn(low, linv)
         for i in range(4):
-            spart[i, DTW : DTW + 16, :] = g[i * 16 : i * 16 + 16, :]
-
-    plane_sum(full2, [dtw_grad, finish_early, finish_wz, nothing])
+            spart[i, A_DTW : A_DTW + 16, :] = g[i * 16 : i * 16 + 16, :]
+            spart[i, A_ALOG : A_ALOG + 4, :] = alg[i * 4 : i * 4 + 4, :]
+            for t in tiles:
+                spart[i, A_DTB : A_DTB + 1, lanes(t)] = jnp.sum(dtb_sum[t], axis=0, keepdims=True)
+                spart[i, A_SKIP : A_SKIP + 1, lanes(t)] = jnp.sum(skip_sum[t], axis=0, keepdims=True)
+        late["za"] = [
+            send(spart.at[toward[d], pl.ds(0, A_ROWS)], srecv.at[d - 1], lines[d]) for d in (1, 2, 3)
+        ]
+
+    def shares():
+        late["gwz"] = share(1, wg_out.at[1, :, chans])
+        for copy in late["za"]:
+            copy.wait_recv()
+        sfull[c] = spart[z, 0:A_ROWS, :] + srecv[0] + srecv[1] + srecv[2]
+        late["ga"] = [send(sfull.at[c], sfull.at[c], peers[p]) for p in (3, 1, 2)]
+
+    second_sum = plane_sum(full2, [small_a, finish_early, finish_z, shares])
 
     pg = slope
 
     def pre_grad(i, carry):
-        mixg = full2[i].astype(BF16)
+        mixg = full2[i]
         back_x = dot(mixg, xp[...])
         new = []
         for t in tiles:
@@ -1066,6 +1123,19 @@
         for j in range(3):
             pg[t, total + j * SUB : total + (j + 1) * SUB, :] = from_after(pg[t, j * SUB : (j + 1) * SUB, :], 0.0)
 
+    mixv = jnp.concatenate([full2[i] for i in range(nblk)], axis=0)
+    actv = jnp.concatenate([tiles_bf(act, i) for i in range(nblk)], axis=0)
+    gx = dot_tn(mixv, actv)
+    for i in range(4):
+        conv_rows = [
+            jnp.concatenate([jnp.sum(conv_sum[5 * t + j], axis=0, keepdims=True) for t in tiles], axis=1)
+            for j in (4, 3, 2, 1, 0)
+        ]
+        bpart[i] = jnp.concatenate(
+            [gx[i * 24 : i * 24 + 24, :]] + conv_rows + [jnp.zeros((3, wide), F32)], axis=0
+        ).astype(BF16)
+    z_b = [send(bpart.at[toward[d]], brecv.at[d - 1], lines[d]) for d in (1, 2, 3)]
+
     def inner_grad(i):
         for t in tiles:
             mine = segp[at8(PAD + i * rb, rb), :]
@@ -1083,34 +1153,22 @@
 
     flush(late["so"][1:] + branch_b)
     late["so"][0].wait()
-    norm_a = start_rows(lambda r: dot_nt(gnat[r, :], w_s[0]) + dot_nt(znat[r, :], w_s[1]))
-
-    mixv = jnp.concatenate([full2[i].astype(BF16) for i in range(nblk)], axis=0)
-    actv = jnp.concatenate([tiles_bf(act, i) for i in range(nblk)], axis=0)
-    gx = dot_tn(mixv, actv)
-    for i in range(4):
-        spart[i, XP : XP + 24, :] = gx[i * 24 : i * 24 + 24, :]
-        spart[i, ALOG : ALOG + 4, :] = alg[i * 4 : i * 4 + 4, :]
-        for t in tiles:
-            for j in range(4):
-                spart[i, CONVW + 3 - j : CONVW + 4 - j, lanes(t)] = jnp.sum(
-                    conv_sum[5 * t + 1 + j], axis=0, keepdims=True
-                )
-            spart[i, CONVB : CONVB + 1, lanes(t)] = jnp.sum(conv_sum[5 * t], axis=0, keepdims=True)
-            spart[i, DTB : DTB + 1, lanes(t)] = jnp.sum(dtb_sum[t], axis=0, keepdims=True)
-            spart[i, SKIP : SKIP + 1, lanes(t)] = jnp.sum(skip_sum[t], axis=0, keepdims=True)
-    z_small = [send(spart.at[toward[d]], srecv.at[d - 1], lines[d]) for d in (1, 2, 3)]
+    norm_a = start_rows(
+        [gnat, znat], lambda rows, cols: dot_nt(rows[0], w_s[0, cols, :]) + dot_nt(rows[1], w_s[1, cols, :])
+    )
 
     norm_b = middle_rows(norm_a)
 
-    for copy in z_small:
+    for copy in z_b:
         copy.wait_recv()
-    sfull[c] = spart[z] + srecv[0] + srecv[1] + srecv[2]
-    g_small = [send(sfull.at[c], sfull.at[c], peers[p]) for p in (3, 1, 2)]
+    v = bpart[z].astype(F32)
+    for d in range(3):
+        v = v + brecv[d].astype(F32)
+    bfull[c] = v.astype(BF16)
+    g_b = [send(bfull.at[c], bfull.at[c], peers[p]) for p in (3, 1, 2)]
 
     v = owned_grad(0, z_wx).T
     gres[0] = v.astype(BF16)
-    late["gwx"] = share(0, wg_out.at[0, :, chans])
     v = late["gain"] + v * w_s[0, zrows, :].astype(F32)
     v = v[:, :LANES] + v[:, LANES:]
     for b in range(block // LANES):
@@ -1120,27 +1178,31 @@
     s_gain += [send(ggs.at[0], ggs.at[3 + p], (z, plane[p], 1 - k)) for p in (1, 2, 3)]
     s_gain.append(send(ggs.at[0], ggs.at[7], sib))
 
+    late["gwx"] = share(0, wg_out.at[0, :, chans])
+
     ng = end_rows(norm_b)
-    rows = pl.ds(pl.multiple_of(k * half, half), half)
-    xv = x_ref[rows, :].astype(F32)
+    xv = x_half[...].astype(F32)
     r = lax.rsqrt(jnp.mean(xv * xv, axis=1, keepdims=True) + EPS)
     sg = ng * gain_row
     sg_s[...] = (
-        og_ref[rows, :].astype(F32) + r * sg - xv * (r * r * r) * jnp.mean(sg * xv, axis=1, keepdims=True)
-    )
-    last = [local(sg_s, sg_out.at[rows, :]), send(sg_s, sg_out.at[rows, :], sib)]
-
-    for copy in g_small:
+        og_half[...].astype(F32) + r * sg - xv * (r * r * r) * jnp.mean(sg * xv, axis=1, keepdims=True)
+    )
+    last = [local(sg_s, sg_out.at[half_rows, :]), send(sg_s, sg_out.at[half_rows, :], sib)]
+
+    for copy in late["ga"] + g_b:
         copy.wait_recv()
     for i in range(4):
-        sm_out[:, i * wide : (i + 1) * wide] = sfull[i]
-    cv_out[...] = sfull[z, CONVW : CONVW + 8, :]
+        cols = slice(i * wide, (i + 1) * wide)
+        sm_out[0:24, cols] = bfull[i, B_XP : B_XP + 24, :].astype(F32)
+        sm_out[24:44, cols] = sfull[i, A_DTW : A_ALOG + 4, :]
+    cv_out[0:5, :] = bfull[z, B_CONVW : B_CONVB + 1, :].astype(F32)
+    cv_out[5:7, :] = sfull[z, A_DTB : A_SKIP + 1, :]
     for copy in s_gain:
         copy.wait_recv()
     v = ggs[0]
     for i in range(1, 8):
         v = v + ggs[i]
-    gg_out[...] = v[0:1, :] / gain_ref[...].astype(F32)
+    gg_out[...] = v[0:1, :] / pk_f[z, GAIN : GAIN + 1, :]
 
     late["so"][1].wait_recv()
     for name in ("gwo", "gwz", "gwx"):
@@ -1166,18 +1228,19 @@
     f, b = (lambda *s: pltpu.VMEM(s, F32)), (lambda *s: pltpu.VMEM(s, BF16))
     scan = f(2, total, LANES)
     scratch = dict(
-        xf=b(total, width), mg=b(total, width), w_s=b(2, width, wide), wo_s=b(wide, width),
+        x_half=b(tok // 2, width), og_half=b(tok // 2, width), xf=b(total, width), mg=b(total, width), w_s=b(2, width, wide), wo_s=b(wide, width),
         pk_f=f(4, ROWS, wide), pk_s=b(4, ROWS, wide), segs=pltpu.VMEM((4, SUB, tok), jnp.int32),
         segp=f(total + 2 * PAD, LANES), maskc=f(tok, LANES), nat=scan, inner=f(2, total + PAD, LANES),
         slope=f(2, total + PAD, LANES), act=scan, gate=scan, dt=scan, yg=scan, y=scan,
         bc=f(2 * states, total, LANES), h=f(2, states, total + SUB, LANES), a2b=f(2, states, SUB, LANES),
         st=f(2, states, SUB, LANES), gin=f(2, states, SUB, LANES), cum=f(2, SUB, LANES), alg=f(states, wide),
-        full=f(8, 128, LANES), full2=f(8, 128, LANES), mp=f(8, 128, LANES), sum_a=f(4, 128, LANES),
-        recv_a=f(4, 128, LANES), recv_b=f(3, 128, LANES), xp=b(LANES, wide), dtwp=b(LANES, wide),
+        full=b(8, 128, LANES), full2=b(8, 128, LANES), mp=f(8, 128, LANES), sum_a=b(4, 128, LANES),
+        recv_a=f(4, 128, LANES), recv_b=b(3, 128, LANES), xp=b(LANES, wide), dtwp=b(LANES, wide),
         big_send=b(4, tok // 2, width), big_keep=b(4, tok // 2, width),
         big_recv=b(4, tok // 2, width), big_rb=b(3, tok // 2, width), gpart=b(2, wide, width),
         zrecv=b(3, 3, wide, block), gres=b(3, block, wide), gnat=b(total, wide), znat=b(total, wide),
-        spart=f(4, ROWS, wide), srecv=f(3, ROWS, wide), sfull=f(4, ROWS, wide), sown=f(ROWS, wide),
+        spart=f(4, ROWS, wide), srecv=f(3, A_ROWS, wide), sfull=f(4, A_ROWS, wide),
+        bpart=b(4, B_ROWS, wide), brecv=b(3, B_ROWS, wide), bfull=b(4, B_ROWS, wide), sown=f(ROWS, wide),
         ggs=f(8, SUB, block), sg_s=f(tok // 2, width),
         ssem=pltpu.SemaphoreType.DMA((112,)), rsem=pltpu.SemaphoreType.DMA((112,)),
         lsem=pltpu.SemaphoreType.DMA((12,)),
@@ -1189,11 +1252,11 @@
             jax.ShapeDtypeStruct((tok, width), F32),
             jax.ShapeDtypeStruct((2, block, 4 * wide), BF16),
             jax.ShapeDtypeStruct((4 * wide, block), BF16),
-            jax.ShapeDtypeStruct((ROWS, 4 * wide), F32),
+            jax.ShapeDtypeStruct((48, 4 * wide), F32),
             jax.ShapeDtypeStruct((8, wide), F32),
             jax.ShapeDtypeStruct((1, block), F32),
         ],
-        in_specs=[vm, vm, hbm, hbm] + [vm] * 10,
+        in_specs=[hbm] * 4 + [vm] * 10,
         out_specs=[hbm] * 4 + [vm] * 3,
         scratch_shapes=list(scratch.values()),
         compiler_params=pltpu.CompilerParams(
@@ -1202,23 +1265,78 @@
     )(
         stream_in.reshape(tok, width), out_grad.reshape(tok, width), in_weight, out_weight, xproj_weight,
         dt_weight, a_log, convolution_weight.reshape(4, block), convolution_bias, step_size_bias,
-        skip_term_scale, norm_gain.reshape(1, block), seg_ids, pad_mask,
-    )
-    so, sg, wg, wo, sm, cv, gg = outs
-    return (
-        so.reshape(1, tok, width),
-        sg.reshape(1, tok, width),
-        gg.reshape(block),
-        wg.astype(F32),
-        wo.astype(F32),
-        sm[XP : XP + 24],
-        sm[DTW : DTW + 16],
-        sm[ALOG : ALOG + 4],
-        cv[0:4].reshape(4, 1, wide),
-        cv[4:5],
-        cv[5:6],
-        cv[6:7],
-    )
+        skip_term_scale, norm_gain, seg_ids, pad_mask,
+    )
+    steps = 2
+    part = tok // steps
+
+    def whole(*shape):
+        return pl.BlockSpec(shape, lambda i: (0,) * len(shape))
+
+    return pl.pallas_call(
+        finish_kernel,
+        grid=(steps,),
+        out_shape=[
+            jax.ShapeDtypeStruct((1, tok, width), BF16),
+            jax.ShapeDtypeStruct((1, tok, width), F32),
+            jax.ShapeDtypeStruct((block,), F32),
+            jax.ShapeDtypeStruct((2, block, 4 * wide), F32),
+            jax.ShapeDtypeStruct((4 * wide, block), F32),
+            jax.ShapeDtypeStruct((24, 4 * wide), F32),
+            jax.ShapeDtypeStruct((16, 4 * wide), F32),
+            jax.ShapeDtypeStruct((4, 4 * wide), F32),
+            jax.ShapeDtypeStruct((4, 1, wide), F32),
+            jax.ShapeDtypeStruct((1, wide), F32),
+            jax.ShapeDtypeStruct((1, wide), F32),
+            jax.ShapeDtypeStruct((1, wide), F32),
+        ],
+        in_specs=[
+            pl.BlockSpec((part, width), lambda i: (i, 0)),
+            pl.BlockSpec((part, width), lambda i: (i, 0)),
+            pl.BlockSpec((2, block // steps, 4 * wide), lambda i: (0, i, 0)),
+            pl.BlockSpec((4 * wide // steps, block), lambda i: (i, 0)),
+            whole(48, 4 * wide),
+            whole(8, wide),
+            whole(1, block),
+        ],
+        out_specs=[
+            pl.BlockSpec((1, part, width), lambda i: (0, i, 0)),
+            pl.BlockSpec((1, part, width), lambda i: (0, i, 0)),
+            whole(block),
+            pl.BlockSpec((2, block // steps, 4 * wide), lambda i: (0, i, 0)),
+            pl.BlockSpec((4 * wide // steps, block), lambda i: (i, 0)),
+            whole(24, 4 * wide),
+            whole(16, 4 * wide),
+            whole(4, 4 * wide),
+            whole(4, 1, wide),
+            whole(1, wide),
+            whole(1, wide),
+            whole(1, wide),
+        ],
+        compiler_params=pltpu.CompilerParams(vmem_limit_bytes=VMEM_LIMIT),
+    )(*outs)
+
+
+def finish_kernel(
+    so_ref, sg_ref, wg_ref, wo_ref, sm_ref, cv_ref, gg_ref,
+    so_out, sg_out, gg_out, wg_out, wo_out, xp_out, dtw_out, alog_out, cw_out, cb_out, dtb_out, skip_out,
+):
+    so_out[0] = so_ref[...]
+    sg_out[0] = sg_ref[...]
+    wg_out[...] = wg_ref[...].astype(F32)
+    wo_out[...] = wo_ref[...].astype(F32)
+
+    @pl.when(pl.program_id(0) == 0)
+    def _():
+        gg_out[...] = gg_ref[0]
+        xp_out[...] = sm_ref[0:24, :]
+        dtw_out[...] = sm_ref[24:40, :]
+        alog_out[...] = sm_ref[40:44, :]
+        for j in range(4):
+            cw_out[j] = cv_ref[j : j + 1, :]
+        cb_out[...] = cv_ref[4:5, :]
+        dtb_out[...] = cv_ref[5:6, :]
+        skip_out[...] = cv_ref[6:7, :]
 
 
 def solution(mesh):

time: 147 us -> 125 us (0.85)
  Pallas kernels: 135 us -> 123 us
  local copies, waits for them, and re-layouts: 6.63 us -> 0 us
  other arithmetic: 3.93 us -> 0 us
    pallas_call x1, Pallas kernels: 135 us -> 119 us  [fused(): pl.pallas_call(fused_kernel, out_shape=[jax.ShapeDtypeStruct((tok, width)...]
    convert_element_type x2 -> x0, other arithmetic: 3.93 us -> none  [the longest x1 2.89 us: fused(): wg.astype(F32)]
    pallas_call x0 -> x1, Pallas kernels: none -> 3.89 us  [fused(): pl.pallas_call(finish_kernel, grid=(steps,), out_shape=[jax.ShapeDtypeStr...]
    unnamed x16 -> x0, local copies, waits for them, and re-layouts: 2.95 us -> none
    slice x4 -> x0, local copies, waits for them, and re-layouts: 2.46 us -> none  [the longest x1 0.65 us: fused(): sm[XP:XP + 24]]
where the time goes in v1:
time: 125 us; the launch traced here: 124 us
  Pallas kernels  123 us (98%)
    pallas_call x1, Pallas kernels, fused(): pl.pallas_call(fused_kernel, out_shape=[jax.ShapeDtypeStruct((tok, width)...  119 us
    pallas_call x1, Pallas kernels, fused(): pl.pallas_call(finish_kernel, grid=(steps,), out_shape=[jax.ShapeDtypeStr...  3.89 us

profile of v1, /device:TPU:25, one launch (start us, length us, event | category | flops | bytes accessed | tf_op | source)
XLA Modules:
  0.0 123.6 jit_solution(2293760885658975156)
XLA Ops:
  0.6 119.0 %shard_map.229 = (bf16[256,1024]{1,0:T(8,128)(2,1)}, f32[256,1024]{1,0:T(8,128)}, bf16[2,256,1024]{2,1,0:T(8,128)(2,1)}, bf16[1024,256]{1,0:T(8,128)(2,1)}, f32[...) custom-call(bf16[256,1024]{1,0:T(8,128)(2,1)} %bitcast.3, bf16[256,1024]{1,0:T(8,128)(2,1)} %bitcast.4, ...), custom_call_target="tpu_custom_call" | custom-call | tf_op jit(solution)/shard_map/pallas_call | solution.py:1248
  119.7 3.9 %shard_map.230 = (bf16[1,256,1024]{2,1,0:T(8,128)(2,1)}, f32[1,256,1024]{2,1,0:T(8,128)}, f32[256]{0:T(256)}, f32[2,256,1024]{2,1,0:T(8,128)}, f32[1024,256]{1,0...) custom-call(bf16[256,1024]{1,0:T(8,128)(2,1)} %get-tuple-element.19., ...), custom_call_target="tpu_custom_call" | custom-call | tf_op jit(solution)/shard_map/pallas_call | solution.py:1276

commit v2 on v1

--- a/solution.py
+++ b/solution.py
@@ -426,7 +426,8 @@
 LANES = 128
 PAD = 24
 ROWS = 64
-XP, DTW, ALOG, CONVW, CONVB, DTB, SKIP, GAIN = 0, 24, 40, 44, 48, 49, 50, 51
+XP, DTW, ALOG, ROWS_P = 0, 24, 40, 48
+CONVW, CONVB, DTB, SKIP, GAIN = 0, 4, 5, 6, 7
 A_DTW, A_ALOG, A_DTB, A_SKIP, A_ROWS = 0, 16, 20, 21, 24
 B_XP, B_CONVW, B_CONVB, B_ROWS = 0, 24, 28, 32
 NT = (((1,), (1,)), ((), ()))
@@ -485,7 +486,7 @@
     x_ref, og_ref, win_ref, wout_ref, xproj_ref, dtw_ref, alog_ref, convw_ref, convb_ref, dtb_ref,
     skip_ref, gain_ref, seg_ref, mask_ref,
     so_out, sg_out, wg_out, wo_out, sm_out, cv_out, gg_out,
-    x_half, og_half, xf, mg, w_s, wo_s, pk_f, pk_s, segs, segp, maskc, nat, inner, slope, act, gate, dt, yg, y,
+    x_half, og_half, xf, mg, w_s, wo_s, early, pk_f, pk_s, segs, segp, maskc, nat, inner, slope, act, gate, dt, yg, y,
     bc, h, a2b, st, gin, cum, alg, full, full2, mp, sum_a, recv_a, recv_b, xp, dtwp,
     big_send, big_keep, big_recv, big_rb, gpart, zrecv, gres, gnat, znat, spart, srecv, sfull, bpart, brecv, bfull, sown, ggs,
     sg_s, ssem, rsem, lsem,
@@ -568,16 +569,16 @@
     spart[0, XP : XP + 24, :] = xproj_ref[:, chans].astype(F32)
     spart[0, DTW : DTW + 16, :] = dtw_ref[:, chans].astype(F32)
     spart[0, ALOG : ALOG + 4, :] = alog_ref[:, chans].astype(F32)
-    spart[0, CONVW : CONVW + 4, :] = convw_ref[...].astype(F32)
-    spart[0, CONVB : CONVB + 1, :] = convb_ref[...].astype(F32)
-    spart[0, DTB : DTB + 1, :] = dtb_ref[...].astype(F32)
-    spart[0, SKIP : SKIP + 1, :] = skip_ref[...].astype(F32)
-    spart[0, GAIN : GAIN + 1, :] = gain_ref[...].astype(F32).reshape(1, block)
-    pk_s[z] = spart[0].astype(BF16)
+    early[z, CONVW : CONVW + 4, :] = convw_ref[...].astype(F32)
+    early[z, CONVB : CONVB + 1, :] = convb_ref[...].astype(F32)
+    early[z, DTB : DTB + 1, :] = dtb_ref[...].astype(F32)
+    early[z, SKIP : SKIP + 1, :] = skip_ref[...].astype(F32)
+    early[z, GAIN : GAIN + 1, :] = gain_ref[...].astype(F32).reshape(1, block)
+    pk_s[z] = spart[0, 0:ROWS_P, :].astype(BF16)
     segs[c] = jnp.broadcast_to(seg_ref[...], (SUB, tok))
     pl.semaphore_wait(barrier, len(everyone))
 
-    s_pack = [send(pk_s.at[z], pk_s.at[z], lines[d]) for d in (1, 2, 3)]
+    s_early = [send(early.at[z], early.at[z], lines[d]) for d in (1, 2, 3)]
     s_seg = [send(segs.at[c], segs.at[c], peers[p]) for p in (1, 2, 3)]
     my_half = pl.ds(pl.multiple_of(c * tok + k * half, half), half)
     s_x = [send(x_ref.at[pl.ds(pl.multiple_of(k * half, half), half)], xf.at[my_half], peers[p]) for p in (3, 1, 2)]
@@ -590,6 +591,7 @@
         ]
 
     s_wx = weight(0)
+    s_pack = [send(pk_s.at[z], pk_s.at[z], lines[d]) for d in (1, 2, 3)]
     own_w = [local(win_ref.at[i, :, chans], w_s.at[i, zrows, :]) for i in (0, 1)]
     zcols = pl.ds(pl.multiple_of(z * block, block), block)
     own_wo = local(wout_ref.at[chans, :], wo_s.at[:, zcols])
@@ -606,6 +608,130 @@
     mcol = jnp.concatenate([maskc[...]] * (width // LANES), axis=1)
     own_og.wait()
     mg[own_rows, :] = (mg[own_rows, :].astype(F32) * mcol).astype(BF16)
+
+    for copy in s_early:
+        copy.wait_recv()
+    gain_row = jnp.concatenate([early[i, GAIN : GAIN + 1, :] for i in range(4)], axis=1)
+    sown[...] = early[c]
+
+    def param(row, t):
+        return sown[row : row + 1, lanes(t)]
+
+    for copy in s_seg:
+        copy.wait_recv()
+    for i in range(4):
+        srow = segs[i, 0:1, :].astype(F32)
+        for b in range(tok // LANES):
+            rows = slice(b * LANES, (b + 1) * LANES)
+            nat[0, i * tok + b * LANES : i * tok + (b + 1) * LANES, :] = jnp.broadcast_to(
+                srow[:, rows], (LANES, LANES)
+            ).T
+
+    def seg_in(tau):
+        segp[at8(PAD + tau * SUB, SUB), :] = nat[0, pl.ds(tau, SUB, stride=steps), :]
+
+    loop(steps, seg_in, 8)
+    sub_row = lax.broadcasted_iota(jnp.int32, (SUB, LANES), 0)
+
+    def from_before(v, fill):
+        return jnp.where(sub_row >= 1, pltpu.roll(v, 1, 0), fill)
+
+    def from_after(v, fill):
+        return jnp.where(sub_row < SUB - 1, pltpu.roll(v, SUB - 1, 0), fill)
+
+    for j in range(3):
+        segp[j * SUB : (j + 1) * SUB, :] = from_before(segp[total + j * SUB : total + (j + 1) * SUB, :], -1.0)
+        segp[PAD + total + j * SUB : PAD + total + (j + 1) * SUB, :] = from_after(
+            segp[PAD + j * SUB : PAD + (j + 1) * SUB, :], -2.0
+        )
+
+    def halves(copies, buf):
+        relays = []
+        for copy, p in zip(copies, (3, 1, 2)):
+            copy.wait_recv()
+            rows = pl.ds(pl.multiple_of(plane[p] * tok + k * half, half), half)
+            relays.append(send(buf.at[rows], buf.at[rows], sib))
+        return relays
+
+    def norm(i):
+        rows = pl.ds(pl.multiple_of(i * rb, rb), rb)
+        v = xf[rows, :].astype(F32)
+        r = lax.rsqrt(jnp.mean(v * v, axis=1, keepdims=True) + EPS)
+        xf[rows, :] = (v * r * gain_row).astype(BF16)
+
+    def project_block(i):
+        rows = pl.ds(pl.multiple_of(i * tok, tok), tok)
+        v = dot(xf[rows, :], w_s[0])
+        for t in tiles:
+            nat[t, rows, :] = v[:, lanes(t)]
+
+    per = tok // rb
+    own_x.wait()
+    loop(per, lambda i: norm(c * per + i))
+    r_x = halves(s_x, xf)
+    for copy in s_wx:
+        copy.wait_recv()
+    own_w[0].wait()
+    s_wz = weight(1)
+    project_block(c)
+    for copy, sent, p in zip(r_x, s_x, (3, 1, 2)):
+        copy.wait_recv()
+        flush([copy])
+        loop(per, lambda i, p=p: norm(plane[p] * per + i))
+        project_block(plane[p])
+
+    def project(which, dst, off):
+        def body(i):
+            v = dot(xf[wide_blk(i), :], w_s[which])
+            for t in tiles:
+                nat[t, wide_blk(i), :] = v[:, lanes(t)]
+
+        loop(total // wb, body)
+        permute_in(dst, off, True)
+
+    def permute_in(dst, off, rounded=False):
+        def body(tau):
+            for t in tiles:
+                v = nat[t, pl.ds(tau, SUB, stride=steps), :]
+                dst[t, at8(off + tau * SUB, SUB), :] = v.astype(BF16).astype(F32) if rounded else v
+
+        loop(steps, body, 8)
+
+    def permute_out(src, dst):
+        def body(i):
+            for s in range(SUB):
+                for t in tiles:
+                    nat[t, at8(s * steps + i * SUB, SUB), :] = src[t, pl.ds(i * SUB * SUB + s, SUB, stride=SUB), :]
+
+        loop(steps // SUB, body)
+
+        def cast(i):
+            dst[blk(i), :] = jnp.concatenate([nat[t, blk(i), :] for t in tiles], axis=1).astype(BF16)
+
+        loop(nblk, cast)
+
+    permute_in(inner, PAD, True)
+    for t in tiles:
+        for j in range(3):
+            inner[t, j * SUB : (j + 1) * SUB, :] = from_before(inner[t, total + j * SUB : total + (j + 1) * SUB, :], 0.0)
+
+    def conv(i):
+        for t in tiles:
+            mine = segp[at8(PAD + i * rb, rb), :]
+            pre = jnp.zeros((rb, LANES), F32) + param(CONVB, t)
+            for j in range(4):
+                window = inner[t, at8(PAD + i * rb - j * SUB, rb), :]
+                if j:
+                    window = jnp.where(segp[at8(PAD + i * rb - j * SUB, rb), :] == mine, window, 0.0)
+                pre = pre + param(CONVW + 3 - j, t) * window
+            s = sigmoid(pre)
+            act[t, blk(i), :] = (pre * s).astype(BF16).astype(F32)
+            slope[t, blk(i), :] = s * (1.0 + pre * (1.0 - s))
+
+    loop(nblk, conv)
+
+    def tiles_bf(ref, i):
+        return jnp.concatenate([ref[t, blk(i), :] for t in tiles], axis=1).astype(BF16)
 
     for copy in s_pack:
         copy.wait_recv()
@@ -621,117 +747,6 @@
     for n in range(states):
         for t in tiles:
             a2b[t, n] = jnp.broadcast_to(a2v[n : n + 1, lanes(t)], (SUB, LANES))
-    gain_row = jnp.concatenate([pk_f[i, GAIN : GAIN + 1, :] for i in range(4)], axis=1)
-    sown[...] = pk_f[c]
-
-    def param(row, t):
-        return sown[row : row + 1, lanes(t)]
-
-    for copy in s_seg:
-        copy.wait_recv()
-    for i in range(4):
-        srow = segs[i, 0:1, :].astype(F32)
-        for b in range(tok // LANES):
-            rows = slice(b * LANES, (b + 1) * LANES)
-            nat[0, i * tok + b * LANES : i * tok + (b + 1) * LANES, :] = jnp.broadcast_to(
-                srow[:, rows], (LANES, LANES)
-            ).T
-
-    def seg_in(tau):
-        segp[at8(PAD + tau * SUB, SUB), :] = nat[0, pl.ds(tau, SUB, stride=steps), :]
-
-    loop(steps, seg_in, 8)
-    sub_row = lax.broadcasted_iota(jnp.int32, (SUB, LANES), 0)
-
-    def from_before(v, fill):
-        return jnp.where(sub_row >= 1, pltpu.roll(v, 1, 0), fill)
-
-    def from_after(v, fill):
-        return jnp.where(sub_row < SUB - 1, pltpu.roll(v, SUB - 1, 0), fill)
-
-    for j in range(3):
-        segp[j * SUB : (j + 1) * SUB, :] = from_before(segp[total + j * SUB : total + (j + 1) * SUB, :], -1.0)
-        segp[PAD + total + j * SUB : PAD + total + (j + 1) * SUB, :] = from_after(
-            segp[PAD + j * SUB : PAD + (j + 1) * SUB, :], -2.0
-        )
-
-    def halves(copies, buf):
-        relays = []
-        for copy, p in zip(copies, (3, 1, 2)):
-            copy.wait_recv()
-            rows = pl.ds(pl.multiple_of(plane[p] * tok + k * half, half), half)
-            relays.append(send(buf.at[rows], buf.at[rows], sib))
-        return relays
-
-    r_x = halves(s_x, xf)
-    own_x.wait()
-
-    for copy in r_x:
-        copy.wait_recv()
-
-    def norm(i):
-        v = xf[blk(i), :].astype(F32)
-        r = lax.rsqrt(jnp.mean(v * v, axis=1, keepdims=True) + EPS)
-        xf[blk(i), :] = (v * r * gain_row).astype(BF16)
-
-    flush(r_x)
-    loop(nblk, norm)
-
-    def project(which, dst, off):
-        def body(i):
-            v = dot(xf[wide_blk(i), :], w_s[which]).astype(BF16).astype(F32)
-            for t in tiles:
-                nat[t, wide_blk(i), :] = v[:, lanes(t)]
-
-        loop(total // wb, body)
-        permute_in(dst, off)
-
-    def permute_in(dst, off):
-        def body(tau):
-            for t in tiles:
-                dst[t, at8(off + tau * SUB, SUB), :] = nat[t, pl.ds(tau, SUB, stride=steps), :]
-
-        loop(steps, body, 8)
-
-    def permute_out(src, dst):
-        def body(i):
-            for s in range(SUB):
-                for t in tiles:
-                    nat[t, at8(s * steps + i * SUB, SUB), :] = src[t, pl.ds(i * SUB * SUB + s, SUB, stride=SUB), :]
-
-        loop(steps // SUB, body)
-
-        def cast(i):
-            dst[blk(i), :] = jnp.concatenate([nat[t, blk(i), :] for t in tiles], axis=1).astype(BF16)
-
-        loop(nblk, cast)
-
-    for copy in s_wx:
-        copy.wait_recv()
-    own_w[0].wait()
-    s_wz = weight(1)
-    project(0, inner, PAD)
-    for t in tiles:
-        for j in range(3):
-            inner[t, j * SUB : (j + 1) * SUB, :] = from_before(inner[t, total + j * SUB : total + (j + 1) * SUB, :], 0.0)
-
-    def conv(i):
-        for t in tiles:
-            mine = segp[at8(PAD + i * rb, rb), :]
-            pre = jnp.zeros((rb, LANES), F32) + param(CONVB, t)
-            for j in range(4):
-                window = inner[t, at8(PAD + i * rb - j * SUB, rb), :]
-                if j:
-                    window = jnp.where(segp[at8(PAD + i * rb - j * SUB, rb), :] == mine, window, 0.0)
-                pre = pre + param(CONVW + 3 - j, t) * window
-            s = sigmoid(pre)
-            act[t, blk(i), :] = (pre * s).astype(BF16).astype(F32)
-            slope[t, blk(i), :] = s * (1.0 + pre * (1.0 - s))
-
-    loop(nblk, conv)
-
-    def tiles_bf(ref, i):
-        return jnp.concatenate([ref[t, blk(i), :] for t in tiles], axis=1).astype(BF16)
 
     def mix(i):
         mp[i] = dot_nt(tiles_bf(act, i), xp[...])
@@ -769,12 +784,12 @@
     late = {}
 
     def send_wo():
-        late["wo"] = [send(wout_ref.at[chans, :], wo_s.at[:, zcols], lines[d]) for d in (1, 2, 3)]
-
-    def gates():
         for copy in s_wz:
             copy.wait_recv()
         own_w[1].wait()
+        late["wo"] = [send(wout_ref.at[chans, :], wo_s.at[:, zcols], lines[d]) for d in (1, 2, 3)]
+
+    def gates():
         project(1, gate, 0)
 
     def nothing():
@@ -785,9 +800,10 @@
 
     def gap():
         send_mg()
+        send_wo()
         gates()
 
-    first_sum = plane_sum(full, [nothing, nothing, send_wo, gap])
+    first_sum = plane_sum(full, [nothing, nothing, nothing, gap])
 
     def steps_of(i):
         arg = dot(full[i], dtwp[...])
@@ -797,17 +813,13 @@
 
     loop(nblk, steps_of)
 
-    ahead = lax.broadcasted_iota(jnp.int32, (LANES, 4 * LANES), 0) - 64
-    ahead = ahead - lax.broadcasted_iota(jnp.int32, (LANES, 4 * LANES), 1) // LANES
-
-    def spread(g):
-        pick = jnp.where(ahead == g * 4, 1.0, 0.0).astype(BF16)
-        for i in range(nblk // 2):
-            v = dot(jnp.concatenate([full[2 * i], full[2 * i + 1]], axis=0), pick)
-            for q in range(4):
-                bc[g * 4 + q, i * 2 * rb : (i + 1) * 2 * rb, :] = v[:, lanes(q)]
-
-    loop(2 * states // 4, spread)
+    flat = full[...].reshape(total, LANES)
+    row = lax.broadcasted_iota(jnp.int32, (LANES, wide), 0)
+    col = lax.broadcasted_iota(jnp.int32, (LANES, wide), 1) // LANES
+    for n in range(0, 2 * states, 2):
+        v = dot(flat, jnp.where(row == 64 + n + col, 1.0, 0.0).astype(BF16))
+        for t in tiles:
+            bc[n + t] = v[:, lanes(t)]
 
     def dts(t, tau):
         v = dt[t, tau_rows(tau), :]
@@ -889,36 +901,36 @@
     def owner_rows(i, q):
         return pl.ds(pl.multiple_of(i * tok + q * half, half), half)
 
-    pieces = ((3, 1, 2, 0),)
+    order = (3, 1, 2, 0)
+    groups = width // wide
+
+    def fill(dst, j, q, lefts, right):
+        cols = slice(j * wide, (j + 1) * wide)
+        there = [plane[p] if p else c for p in order]
+        rows = [jnp.concatenate([left[owner_rows(i, q), :] for i in there], axis=0) for left in lefts]
+        v = right(rows, cols)
+        for i, p in enumerate(order):
+            dst[p, :, cols] = v[i * half : (i + 1) * half, :].astype(BF16)
 
     def start_rows(lefts, right):
-        def fill(dst, group, q):
-            there = [plane[p] if p else c for p in group]
-            rows = [jnp.concatenate([left[owner_rows(i, q), :] for i in there], axis=0) for left in lefts]
-
-            def body(j):
-                cols = pl.ds(pl.multiple_of(j * wide, wide), wide)
-                v = right(rows, cols)
-                for i, p in enumerate(group):
-                    dst[p, :, cols] = v[i * half : (i + 1) * half, :].astype(BF16)
-
-            loop(width // wide, body)
-
         first = []
-        for group in pieces:
-            fill(big_send, group, 1 - k)
-            first += [send(big_send.at[p], big_recv.at[p], sib) for p in group]
-        for group in pieces:
-            fill(big_keep, group, k)
+        for j in range(groups):
+            cols = slice(j * wide, (j + 1) * wide)
+            fill(big_send, j, 1 - k, lefts, right)
+            first.append(send(big_send.at[:, :, cols], big_recv.at[:, :, cols], sib))
         return first
 
-    def middle_rows(first):
+    def middle_rows(first, lefts=None, right=None):
         second = []
-        for copy, p in zip(first, pieces[0]):
-            copy.wait_recv()
-            big_keep[p] = (big_keep[p].astype(F32) + big_recv[p].astype(F32)).astype(BF16)
-            if p:
-                second.append(send(big_keep.at[p], big_rb.at[p - 1], peers[p]))
+        for j in range(groups):
+            cols = slice(j * wide, (j + 1) * wide)
+            if lefts:
+                fill(big_keep, j, k, lefts, right)
+            first[j].wait_recv()
+            for p in order:
+                big_keep[p, :, cols] = (big_keep[p, :, cols].astype(F32) + big_recv[p, :, cols].astype(F32)).astype(BF16)
+                if p:
+                    second.append(send(big_keep.at[p, :, cols], big_rb.at[p - 1, :, cols], peers[p]))
         return second
 
     def end_rows(second):
@@ -929,10 +941,17 @@
             v = v + big_rb[p].astype(F32)
         return v
 
-    branch_a = start_rows([gnat], lambda rows, cols: dot(rows[0], wo_s[:, cols]))
+    def branch_part(rows, cols):
+        return dot(rows[0], wo_s[:, cols])
+
+    branch_a = start_rows([gnat], branch_part)
+    for j in range(groups):
+        fill(big_keep, j, k, [gnat], branch_part)
 
     def weight_grad(slot, left, right):
         gpart[slot % 2] = dot_tn(left[...], right[...]).astype(BF16)
+
+    def spread_grad(slot):
         return [
             send(
                 gpart.at[slot % 2, :, pl.ds(pl.multiple_of(toward[d] * block, block), block)],
@@ -953,8 +972,9 @@
     def share(slot, dst):
         return [local(gres.at[slot], dst)] + [send(gres.at[slot], dst, peers[p]) for p in (3, 1, 2)]
 
-    z_wo = weight_grad(2, gnat, mg)
-    z_wz = weight_grad(1, znat, xf)
+    weight_grad(2, gnat, mg)
+    z_wo = spread_grad(2)
+    weight_grad(1, znat, xf)
 
     for t in tiles:
         if t:
@@ -980,6 +1000,8 @@
     part = states // 2
     for lo in (0, part):
         names = list(range(lo, lo + part))
+        if lo:
+            z_wz = spread_grad(1)
 
         def back(i, carry, names=names, lo=lo):
             grads, acc = carry
@@ -1075,7 +1097,8 @@
     def finish_z():
         v = owned_grad(1, z_wz).T
         gres[1] = v.astype(BF16)
-        late["gain"] = v * w_s[1, zrows, :].astype(F32)
+        v = v * w_s[1, zrows, :].astype(F32)
+        late["gain"] = v[:, :LANES] + v[:, LANES:]
 
     def small_a():
         low = jnp.concatenate([full[i] for i in range(nblk)], axis=0)
@@ -1123,6 +1146,39 @@
         for j in range(3):
             pg[t, total + j * SUB : total + (j + 1) * SUB, :] = from_after(pg[t, j * SUB : (j + 1) * SUB, :], 0.0)
 
+    def inner_grad(i):
+        for t in tiles:
+            mine = segp[at8(PAD + i * rb, rb), :]
+            v = pg[t, blk(i), :] * param(CONVW + 3, t)
+            for j in range(1, 4):
+                later = pg[t, at8(i * rb + j * SUB, rb), :]
+                same = segp[at8(PAD + i * rb + j * SUB, rb), :] == mine
+                v = v + jnp.where(same, later, 0.0) * param(CONVW + 3 - j, t)
+            dsum[t, blk(i), :] = v
+
+    loop(nblk, inner_grad)
+    permute_out(dsum, gnat)
+    flush(z_wo)
+    z_wx = []
+    for q in range(2):
+        gpart[0, q * LANES : (q + 1) * LANES, :] = dot_tn(gnat[:, lanes(q)], xf[...]).astype(BF16)
+        z_wx.append(
+            [
+                send(
+                    gpart.at[0, pl.ds(q * LANES, LANES), pl.ds(pl.multiple_of(toward[d] * block, block), block)],
+                    zrecv.at[0, d - 1, pl.ds(q * LANES, LANES)],
+                    lines[d],
+                )
+                for d in (1, 2, 3)
+            ]
+        )
+
+    flush(late["so"][1:] + branch_b)
+    late["so"][0].wait()
+    def norm_part(rows, cols):
+        return dot_nt(rows[0], w_s[0, cols, :]) + dot_nt(rows[1], w_s[1, cols, :])
+
+    norm_a = start_rows([gnat, znat], norm_part)
     mixv = jnp.concatenate([full2[i] for i in range(nblk)], axis=0)
     actv = jnp.concatenate([tiles_bf(act, i) for i in range(nblk)], axis=0)
     gx = dot_tn(mixv, actv)
@@ -1136,49 +1192,37 @@
         ).astype(BF16)
     z_b = [send(bpart.at[toward[d]], brecv.at[d - 1], lines[d]) for d in (1, 2, 3)]
 
-    def inner_grad(i):
-        for t in tiles:
-            mine = segp[at8(PAD + i * rb, rb), :]
-            v = pg[t, blk(i), :] * param(CONVW + 3, t)
-            for j in range(1, 4):
-                later = pg[t, at8(i * rb + j * SUB, rb), :]
-                same = segp[at8(PAD + i * rb + j * SUB, rb), :] == mine
-                v = v + jnp.where(same, later, 0.0) * param(CONVW + 3 - j, t)
-            dsum[t, blk(i), :] = v
-
-    loop(nblk, inner_grad)
-    permute_out(dsum, gnat)
-    flush(z_wo)
-    z_wx = weight_grad(0, gnat, xf)
-
-    flush(late["so"][1:] + branch_b)
-    late["so"][0].wait()
-    norm_a = start_rows(
-        [gnat, znat], lambda rows, cols: dot_nt(rows[0], w_s[0, cols, :]) + dot_nt(rows[1], w_s[1, cols, :])
-    )
-
-    norm_b = middle_rows(norm_a)
-
-    for copy in z_b:
-        copy.wait_recv()
-    v = bpart[z].astype(F32)
-    for d in range(3):
-        v = v + brecv[d].astype(F32)
-    bfull[c] = v.astype(BF16)
-    g_b = [send(bfull.at[c], bfull.at[c], peers[p]) for p in (3, 1, 2)]
-
-    v = owned_grad(0, z_wx).T
-    gres[0] = v.astype(BF16)
-    v = late["gain"] + v * w_s[0, zrows, :].astype(F32)
-    v = v[:, :LANES] + v[:, LANES:]
+    norm_b = middle_rows(norm_a, [gnat, znat], norm_part)
+    gain_sum = late["gain"]
+    late["gwx"] = [[], []]
+    for q in range(2):
+        for copy in z_wx[q]:
+            copy.wait_recv()
+        rows = slice(q * LANES, (q + 1) * LANES)
+        v = gpart[0, rows, zcols].astype(F32)
+        for d in range(3):
+            v = v + zrecv[0, d, rows, :].astype(F32)
+        v = v.T
+        gres[0, :, rows] = v.astype(BF16)
+        dst = wg_out.at[0, :, pl.ds(pl.multiple_of(c * wide + q * LANES, LANES), LANES)]
+        got = [local(gres.at[0, :, rows], dst)] + [send(gres.at[0, :, rows], dst, peers[p]) for p in (3, 1, 2)]
+        late["gwx"][0].append(got[0])
+        late["gwx"][1].extend(got[1:])
+        gain_sum = gain_sum + v * w_s[0, zrows, rows].astype(F32)
+        if q == 0:
+            for copy in z_b:
+                copy.wait_recv()
+            v = bpart[z].astype(F32)
+            for d in range(3):
+                v = v + brecv[d].astype(F32)
+            bfull[c] = v.astype(BF16)
+            g_b = [send(bfull.at[c], bfull.at[c], peers[p]) for p in (3, 1, 2)]
     for b in range(block // LANES):
-        col = v[b * LANES : (b + 1) * LANES, :].T
+        col = gain_sum[b * LANES : (b + 1) * LANES, :].T
         ggs[0, :, lanes(b)] = jnp.broadcast_to(jnp.sum(col, axis=0, keepdims=True), (SUB, LANES))
     s_gain = [send(ggs.at[0], ggs.at[p], peers[p]) for p in (1, 2, 3)]
     s_gain += [send(ggs.at[0], ggs.at[3 + p], (z, plane[p], 1 - k)) for p in (1, 2, 3)]
     s_gain.append(send(ggs.at[0], ggs.at[7], sib))
-
-    late["gwx"] = share(0, wg_out.at[0, :, chans])
 
     ng = end_rows(norm_b)
     xv = x_half[...].astype(F32)
@@ -1202,13 +1246,17 @@
     v = ggs[0]
     for i in range(1, 8):
         v = v + ggs[i]
-    gg_out[...] = v[0:1, :] / pk_f[z, GAIN : GAIN + 1, :]
+    gg_out[...] = v[0:1, :] / early[z, GAIN : GAIN + 1, :]
 
     late["so"][1].wait_recv()
-    for name in ("gwo", "gwz", "gwx"):
+    for name in ("gwo", "gwz"):
         late[name][0].wait()
         for copy in late[name][1:]:
             copy.wait_recv()
+    for copy in late["gwx"][0]:
+        copy.wait()
+    for copy in late["gwx"][1]:
+        copy.wait_recv()
     last[0].wait()
     last[1].wait_recv()
     flush(list(pending))
@@ -1229,7 +1277,7 @@
     scan = f(2, total, LANES)
     scratch = dict(
         x_half=b(tok // 2, width), og_half=b(tok // 2, width), xf=b(total, width), mg=b(total, width), w_s=b(2, width, wide), wo_s=b(wide, width),
-        pk_f=f(4, ROWS, wide), pk_s=b(4, ROWS, wide), segs=pltpu.VMEM((4, SUB, tok), jnp.int32),
+        early=f(4, SUB, wide), pk_f=f(4, ROWS_P, wide), pk_s=b(4, ROWS_P, wide), segs=pltpu.VMEM((4, SUB, tok), jnp.int32),
         segp=f(total + 2 * PAD, LANES), maskc=f(tok, LANES), nat=scan, inner=f(2, total + PAD, LANES),
         slope=f(2, total + PAD, LANES), act=scan, gate=scan, dt=scan, yg=scan, y=scan,
         bc=f(2 * states, total, LANES), h=f(2, states, total + SUB, LANES), a2b=f(2, states, SUB, LANES),
@@ -1240,10 +1288,10 @@
         big_recv=b(4, tok // 2, width), big_rb=b(3, tok // 2, width), gpart=b(2, wide, width),
         zrecv=b(3, 3, wide, block), gres=b(3, block, wide), gnat=b(total, wide), znat=b(total, wide),
         spart=f(4, ROWS, wide), srecv=f(3, A_ROWS, wide), sfull=f(4, A_ROWS, wide),
-        bpart=b(4, B_ROWS, wide), brecv=b(3, B_ROWS, wide), bfull=b(4, B_ROWS, wide), sown=f(ROWS, wide),
+        bpart=b(4, B_ROWS, wide), brecv=b(3, B_ROWS, wide), bfull=b(4, B_ROWS, wide), sown=f(SUB, wide),
         ggs=f(8, SUB, block), sg_s=f(tok // 2, width),
-        ssem=pltpu.SemaphoreType.DMA((112,)), rsem=pltpu.SemaphoreType.DMA((112,)),
-        lsem=pltpu.SemaphoreType.DMA((12,)),
+        ssem=pltpu.SemaphoreType.DMA((144,)), rsem=pltpu.SemaphoreType.DMA((144,)),
+        lsem=pltpu.SemaphoreType.DMA((16,)),
     )
     outs = pl.pallas_call(
         fused_kernel,

time: 125 us -> 121 us (0.968)
  Pallas kernels: 123 us -> 120 us
    pallas_call x1, Pallas kernels: 119 us -> 116 us  [fused(): pl.pallas_call(fused_kernel, out_shape=[jax.ShapeDtypeStruct((tok, width)...]
where the time goes in v2:
time: 121 us
  Pallas kernels  120 us (99%)
    pallas_call x1, Pallas kernels, fused(): pl.pallas_call(fused_kernel, out_shape=[jax.ShapeDtypeStruct((tok, width)...  116 us
    pallas_call x1, Pallas kernels, fused(): pl.pallas_call(finish_kernel, grid=(steps,), out_shape=[jax.ShapeDtypeStr...  3.89 us

profile of v2, /device:TPU:25, one launch (start us, length us, event | category | flops | bytes accessed | tf_op | source)
XLA Modules:
  0.0 120.8 jit_solution(7191595894994955927)
XLA Ops:
  0.6 116.1 %shard_map.229 = (bf16[256,1024]{1,0:T(8,128)(2,1)}, f32[256,1024]{1,0:T(8,128)}, bf16[2,256,1024]{2,1,0:T(8,128)(2,1)}, bf16[1024,256]{1,0:T(8,128)(2,1)}, f32[...) custom-call(bf16[256,1024]{1,0:T(8,128)(2,1)} %bitcast.3, bf16[256,1024]{1,0:T(8,128)(2,1)} %bitcast.4, ...), custom_call_target="tpu_custom_call" | custom-call | tf_op jit(solution)/shard_map/pallas_call | solution.py:1296
  116.7 3.9 %shard_map.230 = (bf16[1,256,1024]{2,1,0:T(8,128)(2,1)}, f32[1,256,1024]{2,1,0:T(8,128)}, f32[256]{0:T(256)}, f32[2,256,1024]{2,1,0:T(8,128)}, f32[1024,256]{1,0...) custom-call(bf16[256,1024]{1,0:T(8,128)(2,1)} %get-tuple-element.19., ...), custom_call_target="tpu_custom_call" | custom-call | tf_op jit(solution)/shard_map/pallas_call | solution.py:1324

commit v3 on v2

--- a/solution.py
+++ b/solution.py
@@ -697,16 +697,17 @@
 
         loop(steps, body, 8)
 
-    def permute_out(src, dst):
+    def permute_out(src, dst, which=tiles):
         def body(i):
             for s in range(SUB):
-                for t in tiles:
+                for t in which:
                     nat[t, at8(s * steps + i * SUB, SUB), :] = src[t, pl.ds(i * SUB * SUB + s, SUB, stride=SUB), :]
 
         loop(steps // SUB, body)
 
         def cast(i):
-            dst[blk(i), :] = jnp.concatenate([nat[t, blk(i), :] for t in tiles], axis=1).astype(BF16)
+            for t in which:
+                dst[blk(i), lanes(t)] = nat[t, blk(i), :].astype(BF16)
 
         loop(nblk, cast)
 
@@ -838,7 +839,7 @@
             return tuple(new) + (carry[states] + killed,)
 
         zero = jnp.zeros((SUB, LANES), F32)
-        got = lax.fori_loop(0, steps, ends, (zero,) * (states + 1), unroll=4)
+        got = lax.fori_loop(0, steps, ends, (zero,) * (states + 1), unroll=8)
         cum[t] = got[states]
         for n in range(states):
             st[t, n] = prefix_of(got[n], jnp.exp2(got[states] * a2b[t, n]))
@@ -862,7 +863,7 @@
             y[t, tau_rows(tau), :] = (parts[0] + parts[1]) + (parts[2] + parts[3])
             return tuple(new)
 
-        lax.fori_loop(0, steps, forward, tuple(st[t, n] for n in range(states)), unroll=4)
+        lax.fori_loop(0, steps, forward, tuple(st[t, n] for n in range(states)), unroll=8)
 
     for copy in late["mg"] + late["wo"]:
         copy.wait_recv()
@@ -903,6 +904,7 @@
 
     order = (3, 1, 2, 0)
     groups = width // wide
+    turns = (0, 2, 1, 3)
 
     def fill(dst, j, q, lefts, right):
         cols = slice(j * wide, (j + 1) * wide)
@@ -913,33 +915,46 @@
             dst[p, :, cols] = v[i * half : (i + 1) * half, :].astype(BF16)
 
     def start_rows(lefts, right):
-        first = []
-        for j in range(groups):
+        first = {}
+        for j in turns:
             cols = slice(j * wide, (j + 1) * wide)
             fill(big_send, j, 1 - k, lefts, right)
-            first.append(send(big_send.at[:, :, cols], big_recv.at[:, :, cols], sib))
+            first[j] = send(big_send.at[:, :, cols], big_recv.at[:, :, cols], sib)
         return first
 
+    def ways(j):
+        return (1, 2) if j < groups // 2 else (2, 1)
+
     def middle_rows(first, lefts=None, right=None):
-        second = []
-        for j in range(groups):
+        second = {}
+        for j in turns:
             cols = slice(j * wide, (j + 1) * wide)
             if lefts:
                 fill(big_keep, j, k, lefts, right)
             first[j].wait_recv()
             for p in order:
                 big_keep[p, :, cols] = (big_keep[p, :, cols].astype(F32) + big_recv[p, :, cols].astype(F32)).astype(BF16)
-                if p:
-                    second.append(send(big_keep.at[p, :, cols], big_rb.at[p - 1, :, cols], peers[p]))
+            near, far = ways(j)
+            second[j] = [
+                send(big_keep.at[3, :, cols], big_rb.at[1, :, cols], peers[near]),
+                send(big_keep.at[near, :, cols], big_rb.at[0, :, cols], peers[near]),
+            ]
         return second
+
+    def pass_rows(second):
+        third = []
+        for j in turns:
+            cols = slice(j * wide, (j + 1) * wide)
+            near, far = ways(j)
+            second[j][0].wait_recv()
+            big_keep[far, :, cols] = (big_keep[far, :, cols].astype(F32) + big_rb[1, :, cols].astype(F32)).astype(BF16)
+            third.append(send(big_keep.at[far, :, cols], big_rb.at[2, :, cols], peers[far]))
+        return [second[j][1] for j in turns] + third, [second[j][0] for j in turns]
 
     def end_rows(second):
         for copy in second:
             copy.wait_recv()
-        v = big_keep[0].astype(F32)
-        for p in range(3):
-            v = v + big_rb[p].astype(F32)
-        return v
+        return big_keep[0].astype(F32) + big_rb[0].astype(F32) + big_rb[2].astype(F32)
 
     def branch_part(rows, cols):
         return dot(rows[0], wo_s[:, cols])
@@ -989,11 +1004,12 @@
                 for n in range(states)
             )
 
-        got = lax.fori_loop(0, steps, back_ends, (zero,) * states, unroll=4)
+        got = lax.fori_loop(0, steps, back_ends, (zero,) * states, unroll=8)
         for n in range(states):
             gin[t, n] = suffix_of(got[n], jnp.exp2(cum[t] * a2b[t, n]))
 
-    flush(branch_a)
+    flush(branch_a.values())
+    branch_b, branch_sent = pass_rows(branch_b)
     so_s = big_send.at[0]
 
     gsum, dsum = gate, y
@@ -1044,7 +1060,7 @@
             return tuple(new_g), tuple(new_a)
 
         start = tuple(gin[t, n] for n in names for t in tiles)
-        _, acc = lax.fori_loop(0, steps, back, (start, (zero,) * (2 * part)), unroll=2)
+        _, acc = lax.fori_loop(0, steps, back, (start, (zero,) * (2 * part)), unroll=4)
         for q, n in enumerate(names):
             for t in tiles:
                 alg[n : n + 1, lanes(t)] = (
@@ -1125,14 +1141,54 @@
 
     pg = slope
 
-    def pre_grad(i, carry):
-        mixg = full2[i]
-        back_x = dot(mixg, xp[...])
+    flush(z_wo)
+    z_wx = []
+    for t in tiles:
+
+        def pre_grad(i, t=t):
+            v = gsum[t, blk(i), :] + dot(full2[i], xp[:, lanes(t)])
+            pg[t, blk(i), :] = v * pg[t, blk(i), :]
+
+        loop(nblk, pre_grad)
+        for j in range(3):
+            pg[t, total + j * SUB : total + (j + 1) * SUB, :] = from_after(pg[t, j * SUB : (j + 1) * SUB, :], 0.0)
+
+        def inner_grad(i, t=t):
+            mine = segp[at8(PAD + i * rb, rb), :]
+            v = pg[t, blk(i), :] * param(CONVW + 3, t)
+            for j in range(1, 4):
+                later = pg[t, at8(i * rb + j * SUB, rb), :]
+                same = segp[at8(PAD + i * rb + j * SUB, rb), :] == mine
+                v = v + jnp.where(same, later, 0.0) * param(CONVW + 3 - j, t)
+            dsum[t, blk(i), :] = v
+
+        loop(nblk, inner_grad)
+        permute_out(dsum, gnat, (t,))
+        gpart[0, lanes(t), :] = dot_tn(gnat[:, lanes(t)], xf[...]).astype(BF16)
+        z_wx.append(
+            [
+                send(
+                    gpart.at[0, pl.ds(t * LANES, LANES), pl.ds(pl.multiple_of(toward[d] * block, block), block)],
+                    zrecv.at[0, d - 1, pl.ds(t * LANES, LANES)],
+                    lines[d],
+                )
+                for d in (1, 2, 3)
+            ]
+        )
+
+    flush(late["so"][1:] + branch_b + branch_sent)
+    late["so"][0].wait()
+    def norm_part(rows, cols):
+        return dot_nt(rows[0], w_s[0, cols, :]) + dot_nt(rows[1], w_s[1, cols, :])
+
+    norm_a = start_rows([gnat, znat], norm_part)
+    norm_b = middle_rows(norm_a, [gnat, znat], norm_part)
+
+    def conv_grad(i, carry):
         new = []
+        mine = segp[at8(PAD + i * rb, rb), :]
         for t in tiles:
-            v = (gsum[t, blk(i), :] + back_x[:, lanes(t)]) * pg[t, blk(i), :]
-            pg[t, blk(i), :] = v
-            mine = segp[at8(PAD + i * rb, rb), :]
+            v = pg[t, blk(i), :]
             new.append(carry[5 * t] + jnp.sum(v.reshape(rb // SUB, SUB, LANES), axis=0))
             for j in range(4):
                 window = inner[t, at8(PAD + i * rb - j * SUB, rb), :]
@@ -1141,44 +1197,8 @@
                 new.append(carry[5 * t + 1 + j] + jnp.sum((v * window).reshape(rb // SUB, SUB, LANES), axis=0))
         return tuple(new)
 
-    conv_sum = lax.fori_loop(0, nblk, pre_grad, (zero,) * 10)
-    for t in tiles:
-        for j in range(3):
-            pg[t, total + j * SUB : total + (j + 1) * SUB, :] = from_after(pg[t, j * SUB : (j + 1) * SUB, :], 0.0)
-
-    def inner_grad(i):
-        for t in tiles:
-            mine = segp[at8(PAD + i * rb, rb), :]
-            v = pg[t, blk(i), :] * param(CONVW + 3, t)
-            for j in range(1, 4):
-                later = pg[t, at8(i * rb + j * SUB, rb), :]
-                same = segp[at8(PAD + i * rb + j * SUB, rb), :] == mine
-                v = v + jnp.where(same, later, 0.0) * param(CONVW + 3 - j, t)
-            dsum[t, blk(i), :] = v
-
-    loop(nblk, inner_grad)
-    permute_out(dsum, gnat)
-    flush(z_wo)
-    z_wx = []
-    for q in range(2):
-        gpart[0, q * LANES : (q + 1) * LANES, :] = dot_tn(gnat[:, lanes(q)], xf[...]).astype(BF16)
-        z_wx.append(
-            [
-                send(
-                    gpart.at[0, pl.ds(q * LANES, LANES), pl.ds(pl.multiple_of(toward[d] * block, block), block)],
-                    zrecv.at[0, d - 1, pl.ds(q * LANES, LANES)],
-                    lines[d],
-                )
-                for d in (1, 2, 3)
-            ]
-        )
-
-    flush(late["so"][1:] + branch_b)
-    late["so"][0].wait()
-    def norm_part(rows, cols):
-        return dot_nt(rows[0], w_s[0, cols, :]) + dot_nt(rows[1], w_s[1, cols, :])
-
-    norm_a = start_rows([gnat, znat], norm_part)
+    conv_sum = lax.fori_loop(0, nblk, conv_grad, (zero,) * 10)
+    norm_b, _ = pass_rows(norm_b)
     mixv = jnp.concatenate([full2[i] for i in range(nblk)], axis=0)
     actv = jnp.concatenate([tiles_bf(act, i) for i in range(nblk)], axis=0)
     gx = dot_tn(mixv, actv)
@@ -1191,11 +1211,10 @@
             [gx[i * 24 : i * 24 + 24, :]] + conv_rows + [jnp.zeros((3, wide), F32)], axis=0
         ).astype(BF16)
     z_b = [send(bpart.at[toward[d]], brecv.at[d - 1], lines[d]) for d in (1, 2, 3)]
-
-    norm_b = middle_rows(norm_a, [gnat, znat], norm_part)
     gain_sum = late["gain"]
     late["gwx"] = [[], []]
-    for q in range(2):
+
+    def owned_half(q):
         for copy in z_wx[q]:
             copy.wait_recv()
         rows = slice(q * LANES, (q + 1) * LANES)
@@ -1204,34 +1223,40 @@
             v = v + zrecv[0, d, rows, :].astype(F32)
         v = v.T
         gres[0, :, rows] = v.astype(BF16)
+        return v * w_s[0, zrows, rows].astype(F32)
+
+    def share_half(q):
+        rows = slice(q * LANES, (q + 1) * LANES)
         dst = wg_out.at[0, :, pl.ds(pl.multiple_of(c * wide + q * LANES, LANES), LANES)]
-        got = [local(gres.at[0, :, rows], dst)] + [send(gres.at[0, :, rows], dst, peers[p]) for p in (3, 1, 2)]
-        late["gwx"][0].append(got[0])
-        late["gwx"][1].extend(got[1:])
-        gain_sum = gain_sum + v * w_s[0, zrows, rows].astype(F32)
-        if q == 0:
-            for copy in z_b:
-                copy.wait_recv()
-            v = bpart[z].astype(F32)
-            for d in range(3):
-                v = v + brecv[d].astype(F32)
-            bfull[c] = v.astype(BF16)
-            g_b = [send(bfull.at[c], bfull.at[c], peers[p]) for p in (3, 1, 2)]
+        late["gwx"][0].append(local(gres.at[0, :, rows], dst))
+        late["gwx"][1].extend(send(gres.at[0, :, rows], dst, peers[p]) for p in (3, 1, 2))
+
+    gain_sum = gain_sum + owned_half(0)
+    share_half(0)
+    for copy in z_b:
+        copy.wait_recv()
+    v = bpart[z].astype(F32)
+    for d in range(3):
+        v = v + brecv[d].astype(F32)
+    bfull[c] = v.astype(BF16)
+    g_b = [send(bfull.at[c], bfull.at[c], peers[p]) for p in (3, 1, 2)]
+    ng = end_rows(norm_b)
+    xv = x_half[...].astype(F32)
+    r = lax.rsqrt(jnp.mean(xv * xv, axis=1, keepdims=True) + EPS)
+    sg = ng * gain_row
+    sg_s[...] = (
+        og_half[...].astype(F32) + r * sg - xv * (r * r * r) * jnp.mean(sg * xv, axis=1, keepdims=True)
+    )
+    last = [local(sg_s, sg_out.at[half_rows, :]), send(sg_s, sg_out.at[half_rows, :], sib)]
+
+    gain_sum = gain_sum + owned_half(1)
     for b in range(block // LANES):
         col = gain_sum[b * LANES : (b + 1) * LANES, :].T
         ggs[0, :, lanes(b)] = jnp.broadcast_to(jnp.sum(col, axis=0, keepdims=True), (SUB, LANES))
     s_gain = [send(ggs.at[0], ggs.at[p], peers[p]) for p in (1, 2, 3)]
     s_gain += [send(ggs.at[0], ggs.at[3 + p], (z, plane[p], 1 - k)) for p in (1, 2, 3)]
     s_gain.append(send(ggs.at[0], ggs.at[7], sib))
-
-    ng = end_rows(norm_b)
-    xv = x_half[...].astype(F32)
-    r = lax.rsqrt(jnp.mean(xv * xv, axis=1, keepdims=True) + EPS)
-    sg = ng * gain_row
-    sg_s[...] = (
-        og_half[...].astype(F32) + r * sg - xv * (r * r * r) * jnp.mean(sg * xv, axis=1, keepdims=True)
-    )
-    last = [local(sg_s, sg_out.at[half_rows, :]), send(sg_s, sg_out.at[half_rows, :], sib)]
+    share_half(1)
 
     for copy in late["ga"] + g_b:
         copy.wait_recv()

time: 121 us -> 120 us (level); the launches traced: 121 us -> 118 us
  Pallas kernels: 120 us -> 117 us
    pallas_call x1, Pallas kernels: 116 us -> 114 us  [fused(): pl.pallas_call(fused_kernel, out_shape=[jax.ShapeDtypeStruct((tok, width)...]
where the time goes in v3:
time: 120 us; the launch traced here: 118 us
  Pallas kernels  117 us (98%)
    pallas_call x1, Pallas kernels, fused(): pl.pallas_call(fused_kernel, out_shape=[jax.ShapeDtypeStruct((tok, width)...  114 us
    pallas_call x1, Pallas kernels, fused(): pl.pallas_call(finish_kernel, grid=(steps,), out_shape=[jax.ShapeDtypeStr...  3.89 us

profile of v3, /device:TPU:25, one launch (start us, length us, event | category | flops | bytes accessed | tf_op | source)
XLA Modules:
  0.0 118.3 jit_solution(770984666903910819)
XLA Ops:
  0.6 113.6 %shard_map.229 = (bf16[256,1024]{1,0:T(8,128)(2,1)}, f32[256,1024]{1,0:T(8,128)}, bf16[2,256,1024]{2,1,0:T(8,128)(2,1)}, bf16[1024,256]{1,0:T(8,128)(2,1)}, f32[...) custom-call(bf16[256,1024]{1,0:T(8,128)(2,1)} %bitcast.3, bf16[256,1024]{1,0:T(8,128)(2,1)} %bitcast.4, ...), custom_call_target="tpu_custom_call" | custom-call | tf_op jit(solution)/shard_map/pallas_call | solution.py:1321
  114.2 3.9 %shard_map.230 = (bf16[1,256,1024]{2,1,0:T(8,128)(2,1)}, f32[1,256,1024]{2,1,0:T(8,128)}, f32[256]{0:T(256)}, f32[2,256,1024]{2,1,0:T(8,128)}, f32[1024,256]{1,0...) custom-call(bf16[256,1024]{1,0:T(8,128)(2,1)} %get-tuple-element.19., ...), custom_call_target="tpu_custom_call" | custom-call | tf_op jit(solution)/shard_map/pallas_call | solution.py:1349

commit v4 on v3

--- a/solution.py
+++ b/solution.py
@@ -486,7 +486,7 @@
     x_ref, og_ref, win_ref, wout_ref, xproj_ref, dtw_ref, alog_ref, convw_ref, convb_ref, dtb_ref,
     skip_ref, gain_ref, seg_ref, mask_ref,
     so_out, sg_out, wg_out, wo_out, sm_out, cv_out, gg_out,
-    x_half, og_half, xf, mg, w_s, wo_s, early, pk_f, pk_s, segs, segp, maskc, nat, inner, slope, act, gate, dt, yg, y,
+    so_s, x_half, og_half, xf, mg, w_s, wo_s, early, pk_f, pk_s, segs, segp, maskc, nat, inner, slope, act, gate, dt, yg, y,
     bc, h, a2b, st, gin, cum, alg, full, full2, mp, sum_a, recv_a, recv_b, xp, dtwp,
     big_send, big_keep, big_recv, big_rb, gpart, zrecv, gres, gnat, znat, spart, srecv, sfull, bpart, brecv, bfull, sown, ggs,
     sg_s, ssem, rsem, lsem,
@@ -578,10 +578,10 @@
     segs[c] = jnp.broadcast_to(seg_ref[...], (SUB, tok))
     pl.semaphore_wait(barrier, len(everyone))
 
+    my_half = pl.ds(pl.multiple_of(c * tok + k * half, half), half)
+    s_seg = [send(segs.at[c], segs.at[c], peers[p]) for p in (1, 2, 3)]
+    s_x = [send(x_ref.at[pl.ds(pl.multiple_of(k * half, half), half)], xf.at[my_half], peers[p]) for p in (3, 1, 2)]
     s_early = [send(early.at[z], early.at[z], lines[d]) for d in (1, 2, 3)]
-    s_seg = [send(segs.at[c], segs.at[c], peers[p]) for p in (1, 2, 3)]
-    my_half = pl.ds(pl.multiple_of(c * tok + k * half, half), half)
-    s_x = [send(x_ref.at[pl.ds(pl.multiple_of(k * half, half), half)], xf.at[my_half], peers[p]) for p in (3, 1, 2)]
 
     zrows = pl.ds(pl.multiple_of(z * block, block), block)
 
@@ -906,19 +906,22 @@
     groups = width // wide
     turns = (0, 2, 1, 3)
 
-    def fill(dst, j, q, lefts, right):
+    def fill(dst, j, q, lefts, right, more=False):
         cols = slice(j * wide, (j + 1) * wide)
         there = [plane[p] if p else c for p in order]
         rows = [jnp.concatenate([left[owner_rows(i, q), :] for i in there], axis=0) for left in lefts]
         v = right(rows, cols)
         for i, p in enumerate(order):
-            dst[p, :, cols] = v[i * half : (i + 1) * half, :].astype(BF16)
-
-    def start_rows(lefts, right):
+            piece = v[i * half : (i + 1) * half, :]
+            if more:
+                piece = piece + dst[p, :, cols].astype(F32)
+            dst[p, :, cols] = piece.astype(BF16)
+
+    def start_rows(lefts, right, more=False):
         first = {}
         for j in turns:
             cols = slice(j * wide, (j + 1) * wide)
-            fill(big_send, j, 1 - k, lefts, right)
+            fill(big_send, j, 1 - k, lefts, right, more)
             first[j] = send(big_send.at[:, :, cols], big_recv.at[:, :, cols], sib)
         return first
 
@@ -930,7 +933,7 @@
         for j in turns:
             cols = slice(j * wide, (j + 1) * wide)
             if lefts:
-                fill(big_keep, j, k, lefts, right)
+                fill(big_keep, j, k, lefts, right, True)
             first[j].wait_recv()
             for p in order:
                 big_keep[p, :, cols] = (big_keep[p, :, cols].astype(F32) + big_recv[p, :, cols].astype(F32)).astype(BF16)
@@ -1010,7 +1013,6 @@
 
     flush(branch_a.values())
     branch_b, branch_sent = pass_rows(branch_b)
-    so_s = big_send.at[0]
 
     gsum, dsum = gate, y
     part = states // 2
@@ -1137,7 +1139,14 @@
         sfull[c] = spart[z, 0:A_ROWS, :] + srecv[0] + srecv[1] + srecv[2]
         late["ga"] = [send(sfull.at[c], sfull.at[c], peers[p]) for p in (3, 1, 2)]
 
-    second_sum = plane_sum(full2, [small_a, finish_early, finish_z, shares])
+    def norm_z():
+        finish_z()
+        for dst, q in ((big_send, 1 - k), (big_keep, k)):
+            for j in turns:
+                fill(dst, j, q, [znat], lambda rows, cols: dot_nt(rows[0], w_s[1, cols, :]))
+
+    flush(branch_b + branch_sent)
+    second_sum = plane_sum(full2, [small_a, finish_early, norm_z, shares])
 
     pg = slope
 
@@ -1176,13 +1185,13 @@
             ]
         )
 
-    flush(late["so"][1:] + branch_b + branch_sent)
+    flush(late["so"][1:])
     late["so"][0].wait()
     def norm_part(rows, cols):
-        return dot_nt(rows[0], w_s[0, cols, :]) + dot_nt(rows[1], w_s[1, cols, :])
-
-    norm_a = start_rows([gnat, znat], norm_part)
-    norm_b = middle_rows(norm_a, [gnat, znat], norm_part)
+        return dot_nt(rows[0], w_s[0, cols, :])
+
+    norm_a = start_rows([gnat], norm_part, True)
+    norm_b = middle_rows(norm_a, [gnat], norm_part)
 
     def conv_grad(i, carry):
         new = []
@@ -1301,7 +1310,7 @@
     f, b = (lambda *s: pltpu.VMEM(s, F32)), (lambda *s: pltpu.VMEM(s, BF16))
     scan = f(2, total, LANES)
     scratch = dict(
-        x_half=b(tok // 2, width), og_half=b(tok // 2, width), xf=b(total, width), mg=b(total, width), w_s=b(2, width, wide), wo_s=b(wide, width),
+        so_s=b(tok // 2, width), x_half=b(tok // 2, width), og_half=b(tok // 2, width), xf=b(total, width), mg=b(total, width), w_s=b(2, width, wide), wo_s=b(wide, width),
         early=f(4, SUB, wide), pk_f=f(4, ROWS_P, wide), pk_s=b(4, ROWS_P, wide), segs=pltpu.VMEM((4, SUB, tok), jnp.int32),
         segp=f(total + 2 * PAD, LANES), maskc=f(tok, LANES), nat=scan, inner=f(2, total + PAD, LANES),
         slope=f(2, total + PAD, LANES), act=scan, gate=scan, dt=scan, yg=scan, y=scan,

time: 120 us -> 119 us (level)
  no operation moved by 1% of the time
where the time goes in v4:
time: 119 us; the launch traced here: 117 us
  Pallas kernels  116 us (97%)
    pallas_call x1, Pallas kernels, fused(): pl.pallas_call(fused_kernel, out_shape=[jax.ShapeDtypeStruct((tok, width)...  112 us
    pallas_call x1, Pallas kernels, fused(): pl.pallas_call(finish_kernel, grid=(steps,), out_shape=[jax.ShapeDtypeStr...  3.89 us

profile of v4, /device:TPU:25, one launch (start us, length us, event | category | flops | bytes accessed | tf_op | source)
XLA Modules:
  0.0 117.2 jit_solution(10396086387781190480)
XLA Ops:
  0.6 112.5 %shard_map.229 = (bf16[256,1024]{1,0:T(8,128)(2,1)}, f32[256,1024]{1,0:T(8,128)}, bf16[2,256,1024]{2,1,0:T(8,128)(2,1)}, bf16[1024,256]{1,0:T(8,128)(2,1)}, f32[...) custom-call(bf16[256,1024]{1,0:T(8,128)(2,1)} %bitcast.3, bf16[256,1024]{1,0:T(8,128)(2,1)} %bitcast.4, ...), custom_call_target="tpu_custom_call" | custom-call | tf_op jit(solution)/shard_map/pallas_call | solution.py:1330
  113.1 3.9 %shard_map.230 = (bf16[1,256,1024]{2,1,0:T(8,128)(2,1)}, f32[1,256,1024]{2,1,0:T(8,128)}, f32[256]{0:T(256)}, f32[2,256,1024]{2,1,0:T(8,128)}, f32[1024,256]{1,0...) custom-call(bf16[256,1024]{1,0:T(8,128)(2,1)} %get-tuple-element.19., ...), custom_call_target="tpu_custom_call" | custom-call | tf_op jit(solution)/shard_map/pallas_call | solution.py:1358

commit v5 on v4

--- a/solution.py
+++ b/solution.py
@@ -1249,14 +1249,20 @@
         v = v + brecv[d].astype(F32)
     bfull[c] = v.astype(BF16)
     g_b = [send(bfull.at[c], bfull.at[c], peers[p]) for p in (3, 1, 2)]
-    ng = end_rows(norm_b)
-    xv = x_half[...].astype(F32)
-    r = lax.rsqrt(jnp.mean(xv * xv, axis=1, keepdims=True) + EPS)
-    sg = ng * gain_row
-    sg_s[...] = (
-        og_half[...].astype(F32) + r * sg - xv * (r * r * r) * jnp.mean(sg * xv, axis=1, keepdims=True)
-    )
-    last = [local(sg_s, sg_out.at[half_rows, :]), send(sg_s, sg_out.at[half_rows, :], sib)]
+    for copy in norm_b:
+        copy.wait_recv()
+    last = []
+    for q in range(2):
+        part = slice(q * half // 2, (q + 1) * half // 2)
+        ng = big_keep[0, part, :].astype(F32) + big_rb[0, part, :].astype(F32) + big_rb[2, part, :].astype(F32)
+        xv = x_half[part, :].astype(F32)
+        r = lax.rsqrt(jnp.mean(xv * xv, axis=1, keepdims=True) + EPS)
+        sg = ng * gain_row
+        sg_s[part, :] = (
+            og_half[part, :].astype(F32) + r * sg - xv * (r * r * r) * jnp.mean(sg * xv, axis=1, keepdims=True)
+        )
+        there = sg_out.at[pl.ds(pl.multiple_of(k * half + q * half // 2, half // 2), half // 2), :]
+        last.append((local(sg_s.at[part, :], there), send(sg_s.at[part, :], there, sib)))
 
     gain_sum = gain_sum + owned_half(1)
     for b in range(block // LANES):
@@ -1291,8 +1297,9 @@
         copy.wait()
     for copy in late["gwx"][1]:
         copy.wait_recv()
-    last[0].wait()
-    last[1].wait_recv()
+    for copy, sent in last:
+        copy.wait()
+        sent.wait_recv()
     flush(list(pending))
 
 

time: 119 us -> 119 us (level)
  no operation moved by 1% of the time
where the time goes in v5:
time: 119 us; the launch traced here: 117 us
  Pallas kernels  116 us (97%)
    pallas_call x1, Pallas kernels, fused(): pl.pallas_call(fused_kernel, out_shape=[jax.ShapeDtypeStruct((tok, width)...  113 us
    pallas_call x1, Pallas kernels, fused(): pl.pallas_call(finish_kernel, grid=(steps,), out_shape=[jax.ShapeDtypeStr...  3.89 us

profile of v5, /device:TPU:25, one launch (start us, length us, event | category | flops | bytes accessed | tf_op | source)
XLA Modules:
  0.0 117.2 jit_solution(3559743568877217477)
XLA Ops:
  0.6 112.5 %shard_map.229 = (bf16[256,1024]{1,0:T(8,128)(2,1)}, f32[256,1024]{1,0:T(8,128)}, bf16[2,256,1024]{2,1,0:T(8,128)(2,1)}, bf16[1024,256]{1,0:T(8,128)(2,1)}, f32[...) custom-call(bf16[256,1024]{1,0:T(8,128)(2,1)} %bitcast.3, bf16[256,1024]{1,0:T(8,128)(2,1)} %bitcast.4, ...), custom_call_target="tpu_custom_call" | custom-call | tf_op jit(solution)/shard_map/pallas_call | solution.py:1337
  113.2 3.9 %shard_map.230 = (bf16[1,256,1024]{2,1,0:T(8,128)(2,1)}, f32[1,256,1024]{2,1,0:T(8,128)}, f32[256]{0:T(256)}, f32[2,256,1024]{2,1,0:T(8,128)}, f32[1024,256]{1,0...) custom-call(bf16[256,1024]{1,0:T(8,128)(2,1)} %get-tuple-element.19., ...), custom_call_target="tpu_custom_call" | custom-call | tf_op jit(solution)/shard_map/pallas_call | solution.py:1365
